TPU v7x, 256 devices: a whole 4x4x8 slice. The times are simulated.
256 devices in a mesh: lat: 8 (over y_lo, x), lon: 32 (over z, y_hi, core).
Axes of the slice: x: 4, y: 4 (y_hi: 2, y_lo: 2; y = y_hi * 2 + y_lo), z: 8, core: 2. Of those that a mesh axis runs over, the one named last changes fastest.
Arguments:
- tokens: bfloat16 [320, 768, 1024], P('lat', 'lon'), may hold values from -6 to 6
- qkv_weight: bfloat16 [1024, 3072], replicated, may hold values from -3 to 3, as said below
- proj_weight: bfloat16 [1024, 1024], replicated, may hold values from -0.1875 to 0.1875
Outputs:
- mixed: bfloat16 [320, 768, 1024], P('lat', 'lon')
Inputs may be any that keep to these rules, and one draw needn't show every extreme that they name: `qkv_weight`: columns hold the query, key and value projections in that order, heads in order within each.
All inputs are finite; a program needn't handle non-finite values.
Results may differ from a plain program's by a relative error of at most 0.0047.
Values may be sent and summed in bfloat16 or wider, within the bound.
A program may use at most 128 MiB of HBM per device.

v0:
```python
import jax
import jax.numpy as jnp
from jax import lax
from jax.sharding import PartitionSpec as P

HEADS = 16
HALO = 2
HD = 64


def extended(cells, sides, width, closed):
    for axis, dim in sides:
        count = lax.axis_size(axis)
        ends = count if closed else count - 1
        head = lax.slice_in_dim(cells, 0, width, axis=dim)
        tail = lax.slice_in_dim(cells, cells.shape[dim] - width, cells.shape[dim], axis=dim)
        cells = jnp.concatenate(
            [
                lax.ppermute(tail, axis, [(i, (i + 1) % count) for i in range(ends)]),
                cells,
                lax.ppermute(head, axis, [((i + 1) % count, i) for i in range(ends)]),
            ],
            axis=dim,
        )
    return cells


def layer_norm(values):
    mean = jnp.mean(values, axis=-1, keepdims=True)
    centered = values - mean
    variance = jnp.mean(centered * centered, axis=-1, keepdims=True)
    return centered * lax.rsqrt(variance + 1e-05)


def extend(data):
    taller = extended(data, (("lat", 0),), HALO, False)
    return extended(taller, (("lon", 1),), HALO, True)


def attend(queries, pairs, valid, width):
    groups = HEADS // 2
    query_groups = queries.reshape(-1, groups, 2 * HD).transpose(1, 0, 2)
    key_groups = pairs[:, :width].reshape(-1, groups, 2 * HD).transpose(1, 0, 2)
    value_groups = pairs[:, width:].reshape(-1, groups, 2 * HD).transpose(1, 0, 2)

    def one_group(items):
        query_part, key_part, value_part = items
        query_heads = query_part.reshape(-1, 2, HD)
        key_heads = key_part.reshape(-1, 2, HD)
        value_heads = value_part.reshape(-1, 2, HD)
        scores = jnp.einsum(
            "qhd,khd->hqk", query_heads, key_heads, preferred_element_type=jnp.float32
        ) * HD ** (-0.5)
        scores = jnp.where(valid[None, None, :], scores, -1e30)
        top = jnp.max(scores, axis=-1, keepdims=True)
        expo = jnp.exp(scores - top)
        weights = (expo / jnp.sum(expo, axis=-1, keepdims=True)).astype(jnp.bfloat16)
        context = jnp.einsum(
            "hqk,khd->qhd", weights, value_heads, preferred_element_type=jnp.float32
        )
        return context.reshape(-1, 2 * HD).astype(jnp.bfloat16)

    outputs = lax.map(one_group, (query_groups, key_groups, value_groups))
    return outputs.transpose(1, 0, 2).reshape(-1, width)


def local(tokens, qkv_weight, proj_weight):
    tile_rows, tile_cols, width = tokens.shape
    lat_index = lax.axis_index("lat")
    lat_count = lax.axis_size("lat")
    own = tokens.astype(jnp.float32).reshape(-1, width)
    normed = layer_norm(own).astype(jnp.bfloat16)
    queries = jnp.dot(normed, qkv_weight[:, :width], preferred_element_type=jnp.float32).astype(
        jnp.bfloat16
    )
    pairs = jnp.dot(normed, qkv_weight[:, width:], preferred_element_type=jnp.float32).astype(
        jnp.bfloat16
    )
    window = extend(pairs.reshape(tile_rows, tile_cols, 2 * width)).reshape(-1, 2 * width)
    row_ids = lat_index * tile_rows + jnp.arange(tile_rows + 2 * HALO, dtype=jnp.int32) - HALO
    valid_rows = (row_ids >= 0) & (row_ids < lat_count * tile_rows)
    valid = jnp.repeat(valid_rows, tile_cols + 2 * HALO)
    context = attend(queries, window, valid, width)
    mixed = (own + jnp.dot(context, proj_weight, preferred_element_type=jnp.float32)).astype(
        jnp.bfloat16
    )
    return mixed.reshape(tile_rows, tile_cols, width)


def solution(mesh):
    in_specs = (P("lat", "lon", None), P(), P())
    out_specs = P("lat", "lon", None)
    return jax.shard_map(local, mesh=mesh, in_specs=in_specs, out_specs=out_specs, check_vma=False)
```

profile of v0, /device:TPU:2, one launch (start us, length us, event | category | flops | bytes accessed | tf_op | source)
XLA Modules:
  0.0 163.9 jit_solution(1691596508570544838)
XLA Ops:
  6.5 6.7 %fusion.25 = bf16[960,2048]{1,0:T(8,128)(2,1)S(1)} fusion(bf16[960,1024]{1,0:T(8,128)(2,1)S(1)} %fusion.23, bf16[1024,3072]{1,0:T(8,128)(2,1)} %param.6), kind=kOutput, calls=%fused_computation.33 | convolution fusion | flops 4028497920 | bytes 10092544 | tf_op jit(solution)/shard_map/dot_general | solution.py:76
  25.6 6.8 %collective-permute-start.3 = (bf16[44,2,2048]{2,1,0:T(2,128)(2,1)S(1)}, bf16[44,2,2048]{2,1,0:T(2,128)(2,1)}, u32[]{:S(2)}, u32[]{:S(2)}) collective-permute-start(bf16[44,2,2048]{2,1,0:T(2,128)(2,1)S(1)} %get-tuple-element.70), channel_id=1, source_target_pairs={{1,0},{2,1},{3,2},{4,3},{5,4},{6,5},{7,6},{8,7},{9,8},{10,9},{11,1... | collective-permute-start | bytes 1081352 | tf_op jit(solution)/shard_map/ppermute | solution.py:21
  32.4 5.1 %fusion.30 = bf16[960,1024]{1,0:T(8,128)(2,1)} fusion(bf16[960,1024]{1,0:T(8,128)(2,1)S(1)} %fusion.23, bf16[1024,3072]{1,0:T(8,128)(2,1)} %param.6), kind=kOutput, calls=%fused_computation.36 | convolution fusion | flops 2014248960 | bytes 6029312 | tf_op jit(solution)/shard_map/dot_general | solution.py:73
  37.5 3.9 %copy.11 = bf16[960,1024]{0,1:T(8,128)(2,1)} copy(bf16[960,1024]{1,0:T(8,128)(2,1)} %fusion.30) | data formatting | bytes 3932160 | tf_op jit(solution)/shard_map/reshape | solution.py:42
  41.4 9.0 %pad_maximum_fusion = bf16[44,28,2048]{2,1,0:T(8,128)(2,1)} fusion(bf16[44,2,2048]{2,1,0:T(2,128)(2,1)} %collective-permute-done.3, bf16[2,24,2048]{2,1,0:T(8,128)(2,1)S(1)} %collective-permute-done.1, bf16[40,24,2048]{2,1,0:T(8,128)(2,1)} %bitcast.59, bf16[2,24,2048]{2,1,0:T(8,128)(2,1)S(1)} %collective-permute-done, ...), kind=kLoop, calls=%fused_computation.21 | loop fusion | flops 25231360 | bytes 10092544 | tf_op jit(solution)/shard_map/concatenate | solution.py:17
  50.4 7.7 %reshape.87 = bf16[1232,2048]{1,0:T(8,128)(2,1)} reshape(bf16[44,28,2048]{2,1,0:T(8,128)(2,1)} %pad_maximum_fusion) | data formatting | bytes 10092544 | tf_op jit(solution)/shard_map/reshape | solution.py:79
  58.1 5.3 %fusion.34 = (bf16[1232,1024]{1,0:T(8,128)(2,1)}, bf16[1232,1024]{1,0:T(8,128)(2,1)}) fusion(bf16[1232,2048]{1,0:T(8,128)(2,1)} %reshape.87), kind=kLoop, calls=%fused_computation.44 | loop fusion | bytes 10092544 | tf_op jit(solution)/shard_map/slice | solution.py:43
  63.3 4.4 %copy.10 = bf16[1232,1024]{0,1:T(8,128)(2,1)} copy(bf16[1232,1024]{1,0:T(8,128)(2,1)} %get-tuple-element.68) | data formatting | bytes 5046272 | tf_op jit(solution)/shard_map/reshape | solution.py:44
  67.7 4.4 %copy.12 = bf16[1232,1024]{0,1:T(8,128)(2,1)} copy(bf16[1232,1024]{1,0:T(8,128)(2,1)} %get-tuple-element.67) | data formatting | bytes 5046272 | tf_op jit(solution)/shard_map/reshape | solution.py:43
  72.1 86.1 %while.11 = (s32[]{:T(128)}, bf16[8,960,128]{1,2,0:T(8,128)(2,1)}, bf16[8,1232,128]{1,2,0:T(8,128)(2,1)}, bf16[8,960,128]{1,2,0:T(8,128)(2,1)}, bf16[8,1232,128]...) while((s32[]{:T(128)}, bf16[8,960,128]{1,2,0:T(8,128)(2,1)}, ...), condition=%wide.region_5.6_spmd.clone, body=%wide.region_2.5_spmd.clone.sunk | while | flops 929745152 | bytes 3966609 | solution.py:63
  78.0 4.2 %fusion.58 = bf16[2,64,960]{2,1,0:T(8,128)(2,1)S(1)} fusion(bf16[1232,2,64]{0,2,1:T(8,128)(2,1)S(1)} %bitcast.62, f32[2,960]{1,0:T(2,128)S(1)} %fusion.57, pred[1232]{0:T(1024)(128)(4,1)S(1)} %broadcast_in_dim.68, bf16[960,2,64]{0,2,1:T(8,128)(2,1)S(1)} %bitcast.66, bf16[1232,2,64]{0,2,1:T(8,128)(2,1)S(1)} %bitcast.61), kind=kOutput, calls=%fused_computation.11.clone.1 | convolution fusion | flops 617505856 | bytes 1131216 | tf_op jit(solution)/shard_map/while/body/eval_jaxpr/hqk,khd->qhd/dot_general | solution.py:58
  85.2 3.6 %fusion.57 = f32[2,960]{1,0:T(2,128)S(1)} fusion(pred[1232]{0:T(1024)(128)(4,1)S(1)} %broadcast_in_dim.68, bf16[960,2,64]{0,2,1:T(8,128)(2,1)S(1)} %bitcast.65, bf16[1232,2,64]{0,2,1:T(8,128)(2,1)S(1)} %bitcast.60), kind=kOutput, calls=%fused_computation.43.clone.1 | convolution fusion | flops 312239296 | bytes 570064 | tf_op jit(solution)/shard_map/while/body/eval_jaxpr/sub | solution.py:56
  88.7 4.2 %fusion.58 = bf16[2,64,960]{2,1,0:T(8,128)(2,1)S(1)} fusion(bf16[1232,2,64]{0,2,1:T(8,128)(2,1)S(1)} %bitcast.62, f32[2,960]{1,0:T(2,128)S(1)} %fusion.57, pred[1232]{0:T(1024)(128)(4,1)S(1)} %broadcast_in_dim.68, bf16[960,2,64]{0,2,1:T(8,128)(2,1)S(1)} %bitcast.66, bf16[1232,2,64]{0,2,1:T(8,128)(2,1)S(1)} %bitcast.61), kind=kOutput, calls=%fused_computation.11.clone.1 | convolution fusion | flops 617505856 | bytes 1131216 | tf_op jit(solution)/shard_map/while/body/eval_jaxpr/hqk,khd->qhd/dot_general | solution.py:58
  95.9 3.6 %fusion.57 = f32[2,960]{1,0:T(2,128)S(1)} fusion(pred[1232]{0:T(1024)(128)(4,1)S(1)} %broadcast_in_dim.68, bf16[960,2,64]{0,2,1:T(8,128)(2,1)S(1)} %bitcast.65, bf16[1232,2,64]{0,2,1:T(8,128)(2,1)S(1)} %bitcast.60), kind=kOutput, calls=%fused_computation.43.clone.1 | convolution fusion | flops 312239296 | bytes 570064 | tf_op jit(solution)/shard_map/while/body/eval_jaxpr/sub | solution.py:56
  99.5 4.2 %fusion.58 = bf16[2,64,960]{2,1,0:T(8,128)(2,1)S(1)} fusion(bf16[1232,2,64]{0,2,1:T(8,128)(2,1)S(1)} %bitcast.62, f32[2,960]{1,0:T(2,128)S(1)} %fusion.57, pred[1232]{0:T(1024)(128)(4,1)S(1)} %broadcast_in_dim.68, bf16[960,2,64]{0,2,1:T(8,128)(2,1)S(1)} %bitcast.66, bf16[1232,2,64]{0,2,1:T(8,128)(2,1)S(1)} %bitcast.61), kind=kOutput, calls=%fused_computation.11.clone.1 | convolution fusion | flops 617505856 | bytes 1131216 | tf_op jit(solution)/shard_map/while/body/eval_jaxpr/hqk,khd->qhd/dot_general | solution.py:58
  106.7 3.6 %fusion.57 = f32[2,960]{1,0:T(2,128)S(1)} fusion(pred[1232]{0:T(1024)(128)(4,1)S(1)} %broadcast_in_dim.68, bf16[960,2,64]{0,2,1:T(8,128)(2,1)S(1)} %bitcast.65, bf16[1232,2,64]{0,2,1:T(8,128)(2,1)S(1)} %bitcast.60), kind=kOutput, calls=%fused_computation.43.clone.1 | convolution fusion | flops 312239296 | bytes 570064 | tf_op jit(solution)/shard_map/while/body/eval_jaxpr/sub | solution.py:56
  110.3 4.2 %fusion.58 = bf16[2,64,960]{2,1,0:T(8,128)(2,1)S(1)} fusion(bf16[1232,2,64]{0,2,1:T(8,128)(2,1)S(1)} %bitcast.62, f32[2,960]{1,0:T(2,128)S(1)} %fusion.57, pred[1232]{0:T(1024)(128)(4,1)S(1)} %broadcast_in_dim.68, bf16[960,2,64]{0,2,1:T(8,128)(2,1)S(1)} %bitcast.66, bf16[1232,2,64]{0,2,1:T(8,128)(2,1)S(1)} %bitcast.61), kind=kOutput, calls=%fused_computation.11.clone.1 | convolution fusion | flops 617505856 | bytes 1131216 | tf_op jit(solution)/shard_map/while/body/eval_jaxpr/hqk,khd->qhd/dot_general | solution.py:58
  117.5 3.6 %fusion.57 = f32[2,960]{1,0:T(2,128)S(1)} fusion(pred[1232]{0:T(1024)(128)(4,1)S(1)} %broadcast_in_dim.68, bf16[960,2,64]{0,2,1:T(8,128)(2,1)S(1)} %bitcast.65, bf16[1232,2,64]{0,2,1:T(8,128)(2,1)S(1)} %bitcast.60), kind=kOutput, calls=%fused_computation.43.clone.1 | convolution fusion | flops 312239296 | bytes 570064 | tf_op jit(solution)/shard_map/while/body/eval_jaxpr/sub | solution.py:56
  121.0 4.2 %fusion.58 = bf16[2,64,960]{2,1,0:T(8,128)(2,1)S(1)} fusion(bf16[1232,2,64]{0,2,1:T(8,128)(2,1)S(1)} %bitcast.62, f32[2,960]{1,0:T(2,128)S(1)} %fusion.57, pred[1232]{0:T(1024)(128)(4,1)S(1)} %broadcast_in_dim.68, bf16[960,2,64]{0,2,1:T(8,128)(2,1)S(1)} %bitcast.66, bf16[1232,2,64]{0,2,1:T(8,128)(2,1)S(1)} %bitcast.61), kind=kOutput, calls=%fused_computation.11.clone.1 | convolution fusion | flops 617505856 | bytes 1131216 | tf_op jit(solution)/shard_map/while/body/eval_jaxpr/hqk,khd->qhd/dot_general | solution.py:58
  131.8 4.2 %fusion.58 = bf16[2,64,960]{2,1,0:T(8,128)(2,1)S(1)} fusion(bf16[1232,2,64]{0,2,1:T(8,128)(2,1)S(1)} %bitcast.62, f32[2,960]{1,0:T(2,128)S(1)} %fusion.57, pred[1232]{0:T(1024)(128)(4,1)S(1)} %broadcast_in_dim.68, bf16[960,2,64]{0,2,1:T(8,128)(2,1)S(1)} %bitcast.66, bf16[1232,2,64]{0,2,1:T(8,128)(2,1)S(1)} %bitcast.61), kind=kOutput, calls=%fused_computation.11.clone.1 | convolution fusion | flops 617505856 | bytes 1131216 | tf_op jit(solution)/shard_map/while/body/eval_jaxpr/hqk,khd->qhd/dot_general | solution.py:58
  142.6 4.2 %fusion.58 = bf16[2,64,960]{2,1,0:T(8,128)(2,1)S(1)} fusion(bf16[1232,2,64]{0,2,1:T(8,128)(2,1)S(1)} %bitcast.62, f32[2,960]{1,0:T(2,128)S(1)} %fusion.57, pred[1232]{0:T(1024)(128)(4,1)S(1)} %broadcast_in_dim.68, bf16[960,2,64]{0,2,1:T(8,128)(2,1)S(1)} %bitcast.66, bf16[1232,2,64]{0,2,1:T(8,128)(2,1)S(1)} %bitcast.61), kind=kOutput, calls=%fused_computation.11.clone.1 | convolution fusion | flops 617505856 | bytes 1131216 | tf_op jit(solution)/shard_map/while/body/eval_jaxpr/hqk,khd->qhd/dot_general | solution.py:58
  149.7 3.6 %fusion.57 = f32[2,960]{1,0:T(2,128)S(1)} fusion(pred[1232]{0:T(1024)(128)(4,1)S(1)} %broadcast_in_dim.68, bf16[960,2,64]{0,2,1:T(8,128)(2,1)S(1)} %bitcast.65, bf16[1232,2,64]{0,2,1:T(8,128)(2,1)S(1)} %bitcast.60), kind=kOutput, calls=%fused_computation.43.clone.1 | convolution fusion | flops 312239296 | bytes 570064 | tf_op jit(solution)/shard_map/while/body/eval_jaxpr/sub | solution.py:56
  153.3 4.2 %fusion.58 = bf16[2,64,960]{2,1,0:T(8,128)(2,1)S(1)} fusion(bf16[1232,2,64]{0,2,1:T(8,128)(2,1)S(1)} %bitcast.62, f32[2,960]{1,0:T(2,128)S(1)} %fusion.57, pred[1232]{0:T(1024)(128)(4,1)S(1)} %broadcast_in_dim.68, bf16[960,2,64]{0,2,1:T(8,128)(2,1)S(1)} %bitcast.66, bf16[1232,2,64]{0,2,1:T(8,128)(2,1)S(1)} %bitcast.61), kind=kOutput, calls=%fused_computation.11.clone.1 | convolution fusion | flops 617505856 | bytes 1131216 | tf_op jit(solution)/shard_map/while/body/eval_jaxpr/hqk,khd->qhd/dot_general | solution.py:58
  158.2 5.7 %fusion.24 = bf16[960,1024]{1,0:T(8,128)(2,1)} fusion(bf16[40,24,1024]{2,1,0:T(8,128)(2,1)} %param.5, bf16[960,1024]{0,1:T(8,128)(2,1)} %bitcast.71, bf16[1024,1024]{1,0:T(8,128)(2,1)S(1)} %copy-done), kind=kOutput, calls=%fused_computation.32 | convolution fusion | flops 2016215040 | bytes 7995392 | tf_op jit(solution)/shard_map/dot_general | solution.py:84
  (65 shorter events, 53.6 us)
Async XLA Ops:
  0.0 158.2 %copy-start = (bf16[1024,1024]{1,0:T(8,128)(2,1)S(1)}, bf16[1024,1024]{1,0:T(8,128)(2,1)}, u32[]{:S(2)}) copy-start(bf16[1024,1024]{1,0:T(8,128)(2,1)} %param.7) | copy-start | bytes 6291460
  13.2 11.7 %copy-start.1 = (bf16[960,2048]{1,0:T(8,128)(2,1)}, bf16[960,2048]{1,0:T(8,128)(2,1)S(1)}, u32[]{:S(2)}) copy-start(bf16[960,2048]{1,0:T(8,128)(2,1)S(1)} %fusion.25) | copy-start | bytes 11796484
  13.2 8.5 %collective-permute-start = (bf16[2,24,2048]{2,1,0:T(8,128)(2,1)S(1)}, bf16[2,24,2048]{2,1,0:T(8,128)(2,1)S(1)}, u32[]{:S(2)}, u32[]{:S(2)}) collective-permute-start(bf16[2,24,2048]{2,1,0:T(8,128)(2,1)S(1)} %bitcast.70), channel_id=1, source_target_pairs={{0,32},{32,64},{64,96},{96,128},{128,160},{160,192},{192,224},{1,3... | collective-permute-start | bytes 589832 | tf_op jit(solution)/shard_map/ppermute | solution.py:19
  16.6 8.3 %collective-permute-start.1 = (bf16[2,24,2048]{2,1,0:T(8,128)(2,1)S(1)}, bf16[2,24,2048]{2,1,0:T(8,128)(2,1)S(1)}, u32[]{:S(2)}, u32[]{:S(2)}) collective-permute-start(bf16[2,24,2048]{2,1,0:T(8,128)(2,1)S(1)} %bitcast.69), channel_id=1, source_target_pairs={{32,0},{64,32},{96,64},{128,96},{160,128},{192,160},{224,192},{33,... | collective-permute-start | bytes 589832 | tf_op jit(solution)/shard_map/ppermute | solution.py:21
  25.5 15.9 %collective-permute-start.2 = (bf16[44,2,2048]{2,1,0:T(2,128)(2,1)S(1)}, bf16[44,2,2048]{2,1,0:T(2,128)(2,1)}, u32[]{:S(2)}, u32[]{:S(2)}) collective-permute-start(bf16[44,2,2048]{2,1,0:T(2,128)(2,1)S(1)} %get-tuple-element.69), channel_id=1, source_target_pairs={{0,1},{1,2},{2,3},{3,4},{4,5},{5,6},{6,7},{7,8},{8,9},{9,10},{10,1... | collective-permute-start | bytes 1081352 | tf_op jit(solution)/shard_map/ppermute | solution.py:19
  25.6 15.8 %collective-permute-start.3 = (bf16[44,2,2048]{2,1,0:T(2,128)(2,1)S(1)}, bf16[44,2,2048]{2,1,0:T(2,128)(2,1)}, u32[]{:S(2)}, u32[]{:S(2)}) collective-permute-start(bf16[44,2,2048]{2,1,0:T(2,128)(2,1)S(1)} %get-tuple-element.70), channel_id=1, source_target_pairs={{1,0},{2,1},{3,2},{4,3},{5,4},{6,5},{7,6},{8,7},{9,8},{10,9},{11,1... | collective-permute-start | bytes 1081352 | tf_op jit(solution)/shard_map/ppermute | solution.py:21
where the time goes:
time: 167 us; the launch traced here: 164 us
  matrix products  79.4 us (48%)
  local copies, waits for them, and re-layouts  49.8 us (30%)
  other arithmetic  15.9 us (10%)
  starting transfers between devices  12.7 us (8%)
  waiting for transfers between devices  5.8 us (3%)
    dot_general x8, matrix products, one_group(): jnp.einsum('hqk,khd->qhd', weights, value_heads, preferred_element_type=j...  33.4 us
    sub x8, matrix products, one_group(): expo = jnp.exp(scores - top)  28.6 us
    dynamic_slice x16, local copies, waits for them, and re-layouts, attend(): outputs = lax.map(one_group, (query_groups, key_groups, value_groups))  16.7 us
    ppermute x2, starting transfers between devices, extended(): lax.ppermute(head, axis, [((i + 1) % count, i) for i in range(ends)])  9.26 us
    concatenate x1, other arithmetic, extended(): jnp.concatenate([lax.ppermute(tail, axis, [(i, (i + 1) % count) for i in...  9.01 us
    reshape x1, local copies, waits for them, and re-layouts, local(): extend(pairs.reshape(tile_rows, tile_cols, 2 * width))  7.69 us
    dot_general x1, matrix products, local(): jnp.dot(normed, qkv_weight[:, width:], preferred_element_type=jnp.float32)  6.65 us
    dynamic_update_slice x8, local copies, waits for them, and re-layouts, attend(): outputs = lax.map(one_group, (query_groups, key_groups, value_groups))  5.8 us
  transfers between devices with their start and end apart: 4, of which 2 were waited for; matrix products, arithmetic and copies ran while one was open for 5% of the time, Pallas kernels for 0%

commit v1 on v0

v1 whole, which is shorter than its diff:
```python
import math

import jax
import jax.numpy as jnp
from jax import lax
from jax.experimental import pallas as pl
from jax.experimental.pallas import tpu as pltpu
from jax.sharding import PartitionSpec as P

D = 1024
HEADS = 16
TH = 40
TW = 24
HALO = 2
HD = 64
OWN = TH * TW
CORNER = 16
SIDE = TH * HALO
CAP = HALO * TW
RIM = 2 * SIDE + 2 * CAP + 4 * CORNER
KEYS = OWN + RIM
CHUNK = 256
PAIRS = HEADS // 2
SCALE = HD ** (-0.5) * math.log2(math.e)
SAFE = 100.0
MESH = pl.DeviceIdType.MESH
F32 = jnp.float32
BF16 = jnp.bfloat16

LEFT, RIGHT, TOP, BOTTOM = 0, SIDE, 2 * SIDE, 2 * SIDE + CAP
CORNERS = 2 * SIDE + 2 * CAP


def picked_rows():
    i = lax.broadcasted_iota(jnp.int32, (2 * SIDE + 4 * CORNER, OWN), 0)
    side = jnp.where(i >= SIDE, i - SIDE, i)
    side_row = (side // 2) * TW + side % 2 + jnp.where(i >= SIDE, TW - HALO, 0)
    j = i - 2 * SIDE
    which = j // CORNER
    c = j % 4
    corner_row = (
        (c // 2) * TW + c % 2 + (which % 2) * (TW - HALO) + (which // 2) * (OWN - CAP)
    )
    return jnp.where(i < 2 * SIDE, side_row, corner_row)


def rim_mask(lat, lats, shape):
    i = lax.broadcasted_iota(jnp.int32, shape, 0)
    corner = (i - CORNERS) // CORNER
    in_corner = i >= CORNERS
    upper = ((i >= TOP) & (i < BOTTOM)) | (in_corner & (corner < 2))
    lower = ((i >= BOTTOM) & (i < CORNERS)) | (in_corner & (corner >= 2))
    bad = in_corner & ((i - CORNERS) % CORNER >= 4)
    bad = bad | (upper & (lat == 0)) | (lower & (lat == lats - 1))
    return jnp.where(bad, 0.0, 1.0).astype(F32)


def project_kernel(lats, lons, tok_hbm, w_hbm, q_hbm, k_hbm, v_hbm, stat_ref,
                   tok, normed, w, edge, rim, qs, ks, vs,
                   tok_sem, w_sem, out_sem, send_sem, recv_sem):
    lat, lon = lax.axis_index("lat"), lax.axis_index("lon")
    up, down = lax.rem(lat + lats - 1, lats), lax.rem(lat + 1, lats)
    west, east = lax.rem(lon + lons - 1, lons), lax.rem(lon + 1, lons)
    barrier = pltpu.get_barrier_semaphore()
    around = [(lat, west), (lat, east), (up, lon), (down, lon),
              (up, west), (up, east), (down, west), (down, east)]
    for device in around:
        pl.semaphore_signal(barrier, inc=1, device_id=device, device_id_type=MESH)

    tok_copy = pltpu.make_async_copy(tok_hbm, tok, tok_sem)
    tok_copy.start()
    w_copies = []
    order = list(range(4, 12)) + list(range(4))
    for c in order:
        cols = pl.ds(c * CHUNK, CHUNK)
        copy = pltpu.make_async_copy(w_hbm.at[:, cols], w.at[c], w_sem.at[c])
        copy.start()
        w_copies.append(copy)
    tok_copy.wait()

    rows = 64
    for r in range(0, OWN, rows):
        x = tok[r:r + rows, :].astype(F32)
        centered = x - jnp.mean(x, axis=-1, keepdims=True)
        var = jnp.mean(centered * centered, axis=-1, keepdims=True)
        normed[r:r + rows, :] = (centered * lax.rsqrt(var + 1e-05)).astype(BF16)

    take = (picked_rows() == lax.broadcasted_iota(jnp.int32, (2 * SIDE + 4 * CORNER, OWN), 1))
    take = jnp.where(take, 1.0, 0.0).astype(BF16)
    edge[...] = jnp.dot(take, normed[...], preferred_element_type=F32).astype(BF16)

    pl.semaphore_wait(barrier, 8)
    e0 = 2 * SIDE
    plan = [
        (edge.at[pl.ds(0, SIDE)], RIGHT, SIDE),
        (edge.at[pl.ds(SIDE, SIDE)], LEFT, SIDE),
        (normed.at[pl.ds(0, CAP)], BOTTOM, CAP),
        (normed.at[pl.ds(OWN - CAP, CAP)], TOP, CAP),
        (edge.at[pl.ds(e0, CORNER)], CORNERS + 3 * CORNER, CORNER),
        (edge.at[pl.ds(e0 + CORNER, CORNER)], CORNERS + 2 * CORNER, CORNER),
        (edge.at[pl.ds(e0 + 2 * CORNER, CORNER)], CORNERS + CORNER, CORNER),
        (edge.at[pl.ds(e0 + 3 * CORNER, CORNER)], CORNERS, CORNER),
    ]
    sends = []
    for n, ((src, at, size), device) in enumerate(zip(plan, around)):
        copy = pltpu.make_async_remote_copy(
            src_ref=src, dst_ref=rim.at[pl.ds(at, size)],
            send_sem=send_sem.at[n], recv_sem=recv_sem.at[n],
            device_id=device, device_id_type=MESH)
        copy.start()
        sends.append(copy)

    def norms(x, row):
        for half in range(2):
            part = x[:, half * 128:half * 128 + 128]
            top = jnp.max(jnp.sum(part * part, axis=1, keepdims=True), axis=0, keepdims=True)
            stat_ref[row + half:row + half + 1, :] = jnp.broadcast_to(top, (1, 128))

    outs = []

    def put(src, dst):
        copy = pltpu.make_async_copy(src, dst, out_sem.at[len(outs)])
        copy.start()
        outs.append(copy)

    for n, c in enumerate(order):
        w_copies[n].wait()
        y = jnp.dot(normed[...], w[c], preferred_element_type=F32)
        cols = slice((c % 4) * CHUNK, (c % 4) * CHUNK + CHUNK)
        at = pl.ds((c % 4) * CHUNK, CHUNK)
        if c < 4:
            y = y * SCALE
            norms(y, 2 * c)
            qs[:, cols] = y.astype(BF16)
            put(qs.at[:, at], q_hbm.at[:, at])
        elif c < 8:
            norms(y, PAIRS + 2 * (c - 4))
            ks[0:OWN, cols] = y.astype(BF16)
            put(ks.at[pl.ds(0, OWN), at], k_hbm.at[pl.ds(0, OWN), at])
        else:
            vs[0:OWN, cols] = y.astype(BF16)
            put(vs.at[pl.ds(0, OWN), at], v_hbm.at[pl.ds(0, OWN), at])

    for copy in sends:
        copy.wait()

    c0 = CORNERS
    stand = normed[0:CAP, :]
    for lo, hi, at_end in ((TOP, BOTTOM, 0), (c0, c0 + 32, 0),
                           (BOTTOM, c0, lats - 1), (c0 + 32, c0 + 64, lats - 1)):
        rim[lo:hi, :] = jnp.where(lat == at_end, stand[0:hi - lo], rim[lo:hi, :])
    mask = rim_mask(lat, lats, (RIM, CHUNK))
    for c in range(4, 12):
        y = jnp.dot(rim[...], w[c], preferred_element_type=F32)
        cols = slice((c % 4) * CHUNK, (c % 4) * CHUNK + CHUNK)
        at = pl.ds((c % 4) * CHUNK, CHUNK)
        if c < 8:
            norms(y, 2 * PAIRS + 2 * (c - 4))
            ks[OWN:KEYS, cols] = y.astype(BF16)
            put(ks.at[pl.ds(OWN, RIM), at], k_hbm.at[pl.ds(OWN, RIM), at])
        else:
            vs[OWN:KEYS, cols] = (y * mask).astype(BF16)
            put(vs.at[pl.ds(OWN, RIM), at], v_hbm.at[pl.ds(OWN, RIM), at])
    for copy in outs:
        copy.wait()


def attend_kernel(lats, lat_ref, stat_ref, q_ref, k_ref, v_ref, tok_hbm, wp_hbm, out_hbm,
                  ones, ctx, tok, wp, out, tok_sem, wp_sem, out_sem):
    g = pl.program_id(0)
    tok_copy = pltpu.make_async_copy(tok_hbm, tok, tok_sem)
    wp_copy = pltpu.make_async_copy(wp_hbm, wp, wp_sem)

    @pl.when(g == 0)
    def _():
        tok_copy.start()
        wp_copy.start()
        ones[0:OWN, :] = jnp.ones((OWN, 128), BF16)
        ones[OWN:KEYS, :] = rim_mask(lat_ref[0], lats, (RIM, 128)).astype(BF16)

    rows = 240
    low = lax.broadcasted_iota(jnp.int32, (1, 128), 1) < HD

    def run(with_top):
        k = k_ref[...]
        v = v_ref[...]
        unit = ones[...]
        va = jnp.where(low, v, unit)
        vb = jnp.where(low, unit, v)
        for r in range(0, OWN, rows):
            q = q_ref[r:r + rows, :]
            zero = jnp.zeros_like(q)
            parts = []
            for h in range(2):
                qh = jnp.where(low, q, zero) if h == 0 else jnp.where(low, zero, q)
                s = lax.dot_general(qh, k, (((1,), (1,)), ((), ())), preferred_element_type=F32)
                if with_top:
                    s = s - jnp.max(s, axis=1, keepdims=True)
                p = jnp.exp2(s).astype(BF16)
                parts.append(jnp.dot(p, va if h == 0 else vb, preferred_element_type=F32))
            total = pltpu.roll(jnp.where(low, parts[1], parts[0]), HD, 1)
            done = jnp.where(low, parts[0], parts[1]) / total
            ctx[g, r:r + rows, :] = done.astype(BF16)

    k_top = jnp.maximum(stat_ref[PAIRS + g, 0], stat_ref[2 * PAIRS + g, 0])
    safe = stat_ref[g, 0] * k_top <= SAFE * SAFE

    @pl.when(safe)
    def _():
        run(False)

    @pl.when(jnp.logical_not(safe))
    def _():
        run(True)

    @pl.when(g == PAIRS - 1)
    def _():
        tok_copy.wait()
        wp_copy.wait()
        copies = []
        for n, r in enumerate(range(0, OWN, rows)):
            context = jnp.concatenate([ctx[p, r:r + rows, :] for p in range(PAIRS)], axis=1)
            y = jnp.dot(context, wp[...], preferred_element_type=F32)
            y = y + tok[r:r + rows, :].astype(F32)
            out[r:r + rows, :] = y.astype(BF16)
            part = pl.ds(r, rows)
            copy = pltpu.make_async_copy(out.at[part], out_hbm.at[part], out_sem.at[n])
            copy.start()
            copies.append(copy)
        for copy in copies:
            copy.wait()


def local(lats, lons, tokens, qkv_weight, proj_weight):
    flat = tokens.reshape(OWN, D)
    any_spec = pl.BlockSpec(memory_space=pl.ANY)
    vm = pltpu.VMEM
    dma = pltpu.SemaphoreType.DMA
    q, k, v, stat = pl.pallas_call(
        lambda *refs: project_kernel(lats, lons, *refs),
        out_shape=[
            jax.ShapeDtypeStruct((OWN, D), BF16),
            jax.ShapeDtypeStruct((KEYS, D), BF16),
            jax.ShapeDtypeStruct((KEYS, D), BF16),
            jax.ShapeDtypeStruct((3 * PAIRS, 128), F32),
        ],
        in_specs=[any_spec, any_spec],
        out_specs=[any_spec, any_spec, any_spec, pl.BlockSpec(memory_space=vm)],
        scratch_shapes=[
            vm((OWN, D), BF16), vm((OWN, D), BF16), vm((12, D, CHUNK), BF16),
            vm((2 * SIDE + 4 * CORNER, D), BF16), vm((RIM, D), BF16),
            vm((OWN, D), BF16), vm((KEYS, D), BF16), vm((KEYS, D), BF16),
            dma(()), dma((12,)), dma((20,)), dma((8,)), dma((8,)),
        ],
        compiler_params=pltpu.CompilerParams(
            collective_id=0, has_side_effects=True, vmem_limit_bytes=56 * 2 ** 20),
    )(flat, qkv_weight)
    lat = lax.axis_index("lat").astype(jnp.int32).reshape(1)
    smem = pl.BlockSpec(memory_space=pltpu.SMEM)
    mixed = pl.pallas_call(
        lambda *refs: attend_kernel(lats, *refs),
        grid=(PAIRS,),
        out_shape=jax.ShapeDtypeStruct((OWN, D), BF16),
        in_specs=[
            smem, smem,
            pl.BlockSpec((OWN, 128), lambda g: (0, g)),
            pl.BlockSpec((KEYS, 128), lambda g: (0, g)),
            pl.BlockSpec((KEYS, 128), lambda g: (0, g)),
            any_spec, any_spec,
        ],
        out_specs=any_spec,
        scratch_shapes=[
            vm((KEYS, 128), BF16), vm((PAIRS, OWN, 128), BF16), vm((OWN, D), BF16),
            vm((D, D), BF16), vm((OWN, D), BF16), dma(()), dma(()), dma((4,)),
        ],
        compiler_params=pltpu.CompilerParams(vmem_limit_bytes=56 * 2 ** 20),
    )(lat, stat, q, k, v, flat, proj_weight)
    return mixed.reshape(TH, TW, D)


def solution(mesh):
    lats, lons = mesh.shape["lat"], mesh.shape["lon"]
    return jax.shard_map(
        lambda *args: local(lats, lons, *args), mesh=mesh,
        in_specs=(P("lat", "lon", None), P(), P()), out_specs=P("lat", "lon", None),
        check_vma=False)
```

time: 167 us -> 66.4 us (0.40); the launches traced: 164 us -> 66.3 us
  matrix products: 79.4 us -> 0 us
  Pallas kernels: 0 us -> 66.1 us
  local copies, waits for them, and re-layouts: 49.8 us -> 0 us
  other arithmetic: 15.9 us -> 0 us
  starting transfers between devices: 12.7 us -> 0 us
  waiting for transfers between devices: 5.8 us -> 0 us
    pallas_call x0 -> x2, Pallas kernels: none -> 66.1 us  [the longest x1 39.2 us: local(): pl.pallas_call(lambda *refs: attend_kernel(lats, *refs), grid=(PAIRS,), o...]
    dot_general x11 -> x0, matrix products: 50.8 us -> none  [the longest x8 33.4 us: one_group(): jnp.einsum('hqk,khd->qhd', weights, value_heads, preferred_element_type=j...]
    sub x8 -> x0, matrix products: 28.6 us -> none  [one_group(): expo = jnp.exp(scores - top)]
    reshape x4 -> x0, local copies, waits for them, and re-layouts: 20.3 us -> none  [the longest x1 7.69 us: local(): extend(pairs.reshape(tile_rows, tile_cols, 2 * width))]
    dynamic_slice x16 -> x0, local copies, waits for them, and re-layouts: 16.7 us -> none  [attend(): outputs = lax.map(one_group, (query_groups, key_groups, value_groups))]
    ppermute x4 -> x0, starting transfers between devices: 12.7 us -> none  [the longest x2 9.26 us: extended(): lax.ppermute(head, axis, [((i + 1) % count, i) for i in range(ends)])]
    concatenate x1 -> x0, other arithmetic: 9.01 us -> none  [extended(): jnp.concatenate([lax.ppermute(tail, axis, [(i, (i + 1) % count) for i in...]
    ppermute x4 -> x0, waiting for transfers between devices: 5.8 us -> none  [the longest x2 3.13 us: extended(): lax.ppermute(head, axis, [((i + 1) % count, i) for i in range(ends)])]
  transfers between devices with their start and end apart: 4 -> 0, of which waited for: 2 -> 0; matrix products, arithmetic and copies ran while one was open for 5% -> 0% of each run, Pallas kernels for 0% -> 0%
where the time goes in v1:
time: 66.4 us; the launch traced here: 66.3 us
  Pallas kernels  66.1 us (100%)
    pallas_call x1, Pallas kernels, local(): pl.pallas_call(lambda *refs: attend_kernel(lats, *refs), grid=(PAIRS,), o...  39.2 us
    pallas_call x1, Pallas kernels, local(): pl.pallas_call(lambda *refs: project_kernel(lats, lons, *refs), out_shape...  27 us

profile of v1, /device:TPU:2, one launch (start us, length us, event | category | flops | bytes accessed | tf_op | source)
XLA Modules:
  0.0 66.3 jit_solution(17615527246950965887)
XLA Ops:
  0.0 27.0 %shard_map.37 = (bf16[960,1024]{1,0:T(8,128)(2,1)}, bf16[1280,1024]{1,0:T(8,128)(2,1)}, bf16[1280,1024]{1,0:T(8,128)(2,1)}, f32[24,128]{1,0:T(8,128)}) custom-call(bf16[960,1024]{1,0:T(8,128)(2,1)} %bitcast.3, bf16[1024,3072]{1,0:T(8,128)(2,1)} %refs_1_.1), custom_call_target="tpu_custom_call" | custom-call | tf_op jit(solution)/shard_map/pallas_call | solution.py:239
  27.0 39.2 %shard_map.38 = bf16[960,1024]{1,0:T(8,128)(2,1)} custom-call(s32[1]{0:T(128)} %bitcast.refs_0_, f32[24,128]{1,0:T(8,128)} %get-tuple-element.9.refs_1_, bf16[960,1024]{1,0:T(8,128)(2,1)} %get-tuple-element.10.refs_2_, bf16[1280,1024]{1,0:T(8,128)(2,1)} %get-tuple-element.11.refs_3_, bf16[1280,1024]{1,0:T(8,128)(2,1)} %get-tuple-element.12.refs_4_, ...), custom_call_target="tpu_custom_call" | custom-call | tf_op jit(solution)/shard_map/pallas_call | solution.py:260

commit v2 on v1

v2 whole, which is shorter than its diff:
```python
import math

import jax
import jax.numpy as jnp
from jax import lax
from jax.experimental import pallas as pl
from jax.experimental.pallas import tpu as pltpu
from jax.sharding import PartitionSpec as P

D = 1024
HEADS = 16
TH = 40
TW = 24
HALO = 2
HD = 64
OWN = TH * TW
CORNER = 16
SIDE = TH * HALO
CAP = HALO * TW
RIM = 2 * SIDE + 2 * CAP + 4 * CORNER
KEYS = OWN + RIM
CHUNK = 512
CHUNKS = 3 * D // CHUNK
QS = D // CHUNK
PAIRS = HEADS // 2
SCALE = HD ** (-0.5) * math.log2(math.e)
SMALL = 2.0 ** -60
LARGE = 2.0 ** 100
MESH = pl.DeviceIdType.MESH
F32 = jnp.float32
BF16 = jnp.bfloat16

LEFT, RIGHT, TOP, BOTTOM = 0, SIDE, 2 * SIDE, 2 * SIDE + CAP
CORNERS = 2 * SIDE + 2 * CAP


def picked_rows():
    i = lax.broadcasted_iota(jnp.int32, (2 * SIDE + 4 * CORNER, OWN), 0)
    side = jnp.where(i >= SIDE, i - SIDE, i)
    side_row = (side // 2) * TW + side % 2 + jnp.where(i >= SIDE, TW - HALO, 0)
    j = i - 2 * SIDE
    which = j // CORNER
    c = j % 4
    corner_row = (
        (c // 2) * TW + c % 2 + (which % 2) * (TW - HALO) + (which // 2) * (OWN - CAP)
    )
    return jnp.where(i < 2 * SIDE, side_row, corner_row)


def rim_mask(lat, lats, shape):
    i = lax.broadcasted_iota(jnp.int32, shape, 0)
    corner = (i - CORNERS) // CORNER
    in_corner = i >= CORNERS
    upper = ((i >= TOP) & (i < BOTTOM)) | (in_corner & (corner < 2))
    lower = ((i >= BOTTOM) & (i < CORNERS)) | (in_corner & (corner >= 2))
    bad = in_corner & ((i - CORNERS) % CORNER >= 4)
    bad = bad | (upper & (lat == 0)) | (lower & (lat == lats - 1))
    return jnp.where(bad, 0.0, 1.0).astype(F32)


def project_kernel(lats, lons, tok_hbm, w_hbm, qkv_hbm,
                   tok, normed, w, edge, rim, res, res_rim,
                   tok_sem, w_sem, own_sem, rim_sem, send_sem, recv_sem):
    lat, lon = lax.axis_index("lat"), lax.axis_index("lon")
    up, down = lax.rem(lat + lats - 1, lats), lax.rem(lat + 1, lats)
    west, east = lax.rem(lon + lons - 1, lons), lax.rem(lon + 1, lons)
    barrier = pltpu.get_barrier_semaphore()
    around = [(lat, west), (lat, east), (up, lon), (down, lon),
              (up, west), (up, east), (down, west), (down, east)]
    for device in around:
        pl.semaphore_signal(barrier, inc=1, device_id=device, device_id_type=MESH)

    rows = 320

    def tok_copy(i):
        part = pl.ds(pl.multiple_of(i * rows, rows), rows)
        return pltpu.make_async_copy(tok_hbm.at[part], tok.at[part], tok_sem.at[i])

    for i in range(OWN // rows):
        tok_copy(i).start()

    def w_copy(c):
        at = pl.ds(pl.multiple_of(c * CHUNK, CHUNK), CHUNK)
        return pltpu.make_async_copy(w_hbm.at[:, at], w.at[c], w_sem.at[c])

    for c in range(CHUNKS):
        w_copy(c).start()

    def norm(i, carry):
        tok_copy(i).wait()
        part = pl.ds(pl.multiple_of(i * rows, rows), rows)
        x = tok[part, :].astype(F32)
        centered = x - jnp.mean(x, axis=-1, keepdims=True)
        var = jnp.mean(centered * centered, axis=-1, keepdims=True)
        normed[part, :] = (centered * lax.rsqrt(var + 1e-05)).astype(BF16)
        return carry

    lax.fori_loop(0, OWN // rows, norm, 0)

    take = (picked_rows() == lax.broadcasted_iota(jnp.int32, (2 * SIDE + 4 * CORNER, OWN), 1))
    take = jnp.where(take, 1.0, 0.0).astype(BF16)
    for c in range(2):
        cols = slice(c * 512, c * 512 + 512)
        edge[:, cols] = jnp.dot(take, normed[:, cols], preferred_element_type=F32).astype(BF16)

    pl.semaphore_wait(barrier, 8)
    e0 = 2 * SIDE
    plan = [
        (edge.at[pl.ds(0, SIDE)], RIGHT, SIDE),
        (edge.at[pl.ds(SIDE, SIDE)], LEFT, SIDE),
        (normed.at[pl.ds(0, CAP)], BOTTOM, CAP),
        (normed.at[pl.ds(OWN - CAP, CAP)], TOP, CAP),
        (edge.at[pl.ds(e0, CORNER)], CORNERS + 3 * CORNER, CORNER),
        (edge.at[pl.ds(e0 + CORNER, CORNER)], CORNERS + 2 * CORNER, CORNER),
        (edge.at[pl.ds(e0 + 2 * CORNER, CORNER)], CORNERS + CORNER, CORNER),
        (edge.at[pl.ds(e0 + 3 * CORNER, CORNER)], CORNERS, CORNER),
    ]
    sends = []
    for n, ((src, at, size), device) in enumerate(zip(plan, around)):
        copy = pltpu.make_async_remote_copy(
            src_ref=src, dst_ref=rim.at[pl.ds(at, size)],
            send_sem=send_sem.at[n], recv_sem=recv_sem.at[n],
            device_id=device, device_id_type=MESH)
        copy.start()
        sends.append(copy)

    def own_out(c):
        return pltpu.make_async_copy(
            res.at[c], qkv_hbm.at[c, pl.ds(0, OWN)], own_sem.at[c])

    def rim_out(c):
        return pltpu.make_async_copy(
            res_rim.at[c - QS], qkv_hbm.at[c, pl.ds(OWN, RIM)], rim_sem.at[c - QS])

    def own(c, carry):
        w_copy(c).wait()
        y = jnp.dot(normed[...], w[c], preferred_element_type=F32)
        y = y * jnp.where(c < QS, SCALE, 1.0)
        res[c] = y.astype(BF16)
        own_out(c).start()
        return carry

    lax.fori_loop(0, CHUNKS, own, 0)

    for copy in sends:
        copy.wait()

    c0 = CORNERS
    stand = normed[0:CAP, :]
    for lo, hi, at_end in ((TOP, BOTTOM, 0), (c0, c0 + 32, 0),
                           (BOTTOM, c0, lats - 1), (c0 + 32, c0 + 64, lats - 1)):
        rim[lo:hi, :] = jnp.where(lat == at_end, stand[0:hi - lo], rim[lo:hi, :])
    mask = rim_mask(lat, lats, (RIM, 128))
    mask = jnp.concatenate([mask] * (CHUNK // 128), axis=1)

    def outer(c, carry):
        y = jnp.dot(rim[...], w[c], preferred_element_type=F32)
        res_rim[c - QS] = (y * jnp.where(c < 2 * QS, 1.0, mask)).astype(BF16)
        rim_out(c).start()
        return carry

    lax.fori_loop(QS, CHUNKS, outer, 0)
    for c in range(CHUNKS):
        own_out(c).wait()
    for c in range(QS, CHUNKS):
        rim_out(c).wait()


def attend_kernel(lats, lat_ref, q_ref, k_ref, v_ref, tok_hbm, wp_hbm, out_hbm,
                  ones, ctx, tok, wp, out, tok_sem, wp_sem, out_sem):
    g = pl.program_id(0)
    tok_copy = pltpu.make_async_copy(tok_hbm, tok, tok_sem)
    wp_copy = pltpu.make_async_copy(wp_hbm, wp, wp_sem)

    @pl.when(g == 0)
    def _():
        tok_copy.start()
        wp_copy.start()
        ones[0:OWN, :] = jnp.ones((OWN, 128), BF16)
        ones[OWN:KEYS, :] = rim_mask(lat_ref[0], lats, (RIM, 128)).astype(BF16)

    rows = 240
    low = lax.broadcasted_iota(jnp.int32, (1, 128), 1) < HD

    def run(with_top):
        k = k_ref[0]
        v = v_ref[0]
        unit = ones[...]
        va = jnp.where(low, v, unit)
        vb = jnp.where(low, unit, v)
        fine = jnp.ones((8, 128), F32)
        for r in range(0, OWN, rows):
            q = q_ref[0, r:r + rows, :]
            zero = jnp.zeros_like(q)
            parts = []
            for h in range(2):
                qh = jnp.where(low, q, zero) if h == 0 else jnp.where(low, zero, q)
                s = lax.dot_general(qh, k, (((1,), (1,)), ((), ())), preferred_element_type=F32)
                if with_top:
                    s = s - jnp.max(s, axis=1, keepdims=True)
                p = jnp.exp2(s).astype(BF16)
                parts.append(jnp.dot(p, va if h == 0 else vb, preferred_element_type=F32))
            total = jnp.where(low, parts[1], parts[0])
            for i in range(0, rows, 8):
                t = total[i:i + 8, :]
                fine = jnp.where((t >= SMALL) & (t <= LARGE), fine, 0.0)
            done = jnp.where(low, parts[0], parts[1]) / pltpu.roll(total, HD, 1)
            ctx[g, r:r + rows, :] = done.astype(BF16)
        return jnp.min(fine) > 0.5

    safe = run(False)

    @pl.when(jnp.logical_not(safe))
    def _():
        run(True)

    @pl.when(g == PAIRS - 1)
    def _():
        tok_copy.wait()
        wp_copy.wait()
        copies = []
        for n, r in enumerate(range(0, OWN, rows)):
            context = jnp.concatenate([ctx[p, r:r + rows, :] for p in range(PAIRS)], axis=1)
            y = jnp.dot(context, wp[...], preferred_element_type=F32)
            y = y + tok[r:r + rows, :].astype(F32)
            out[r:r + rows, :] = y.astype(BF16)
            part = pl.ds(r, rows)
            copy = pltpu.make_async_copy(out.at[part], out_hbm.at[part], out_sem.at[n])
            copy.start()
            copies.append(copy)
        for copy in copies:
            copy.wait()


def local(lats, lons, tokens, qkv_weight, proj_weight):
    flat = tokens.reshape(OWN, D)
    any_spec = pl.BlockSpec(memory_space=pl.ANY)
    vm = pltpu.VMEM
    dma = pltpu.SemaphoreType.DMA
    qkv = pl.pallas_call(
        lambda *refs: project_kernel(lats, lons, *refs),
        out_shape=jax.ShapeDtypeStruct((CHUNKS, KEYS, CHUNK), BF16),
        in_specs=[any_spec, any_spec],
        out_specs=any_spec,
        scratch_shapes=[
            vm((OWN, D), BF16), vm((OWN, D), BF16), vm((CHUNKS, D, CHUNK), BF16),
            vm((2 * SIDE + 4 * CORNER, D), BF16), vm((RIM, D), BF16),
            vm((CHUNKS, OWN, CHUNK), BF16), vm((CHUNKS - QS, RIM, CHUNK), BF16),
            dma((OWN // 320,)), dma((CHUNKS,)), dma((CHUNKS,)), dma((CHUNKS - QS,)), dma((8,)), dma((8,)),
        ],
        compiler_params=pltpu.CompilerParams(
            collective_id=0, has_side_effects=True, vmem_limit_bytes=56 * 2 ** 20),
    )(flat, qkv_weight)
    lat = lax.axis_index("lat").astype(jnp.int32).reshape(1)
    smem = pl.BlockSpec(memory_space=pltpu.SMEM)
    per = CHUNK // 128
    mixed = pl.pallas_call(
        lambda *refs: attend_kernel(lats, *refs),
        grid=(PAIRS,),
        out_shape=jax.ShapeDtypeStruct((OWN, D), BF16),
        in_specs=[
            smem,
            pl.BlockSpec((1, OWN, 128), lambda g: (g // per, 0, g % per)),
            pl.BlockSpec((1, KEYS, 128), lambda g: (QS + g // per, 0, g % per)),
            pl.BlockSpec((1, KEYS, 128), lambda g: (2 * QS + g // per, 0, g % per)),
            any_spec, any_spec,
        ],
        out_specs=any_spec,
        scratch_shapes=[
            vm((KEYS, 128), BF16), vm((PAIRS, OWN, 128), BF16), vm((OWN, D), BF16),
            vm((D, D), BF16), vm((OWN, D), BF16), dma(()), dma(()), dma((4,)),
        ],
        compiler_params=pltpu.CompilerParams(vmem_limit_bytes=56 * 2 ** 20),
    )(lat, qkv, qkv, qkv, flat, proj_weight)
    return mixed.reshape(TH, TW, D)


def solution(mesh):
    lats, lons = mesh.shape["lat"], mesh.shape["lon"]
    return jax.shard_map(
        lambda *args: local(lats, lons, *args), mesh=mesh,
        in_specs=(P("lat", "lon", None), P(), P()), out_specs=P("lat", "lon", None),
        check_vma=False)
```

time: 66.4 us -> 82.2 us (1.24)
  Pallas kernels: 66.1 us -> 81.7 us
    pallas_call x1, Pallas kernels: 39.2 us -> 62.3 us  [local(): pl.pallas_call(lambda *refs: attend_kernel(lats, *refs), grid=(PAIRS,), o...]
    pallas_call x1, Pallas kernels: 27 us -> 19.4 us  [local(): pl.pallas_call(lambda *refs: project_kernel(lats, lons, *refs), out_shape...]
where the time goes in v2:
time: 82.2 us; the launch traced here: 81.8 us
  Pallas kernels  81.7 us (99%)
    pallas_call x1, Pallas kernels, local(): pl.pallas_call(lambda *refs: attend_kernel(lats, *refs), grid=(PAIRS,), o...  62.3 us
    pallas_call x1, Pallas kernels, local(): pl.pallas_call(lambda *refs: project_kernel(lats, lons, *refs), out_shape...  19.4 us

profile of v2, /device:TPU:2, one launch (start us, length us, event | category | flops | bytes accessed | tf_op | source)
XLA Modules:
  0.0 81.8 jit_solution(1405255079638170504)
XLA Ops:
  0.0 19.4 %shard_map.37.refs_1_.refs_2_.refs_3_ = bf16[6,1280,512]{2,1,0:T(8,128)(2,1)} custom-call(bf16[960,1024]{1,0:T(8,128)(2,1)} %bitcast.3, bf16[1024,3072]{1,0:T(8,128)(2,1)} %refs_1_.1), custom_call_target="tpu_custom_call" | custom-call | tf_op jit(solution)/shard_map/pallas_call | solution.py:240
  19.4 62.3 %shard_map.38 = bf16[960,1024]{1,0:T(8,128)(2,1)} custom-call(s32[1]{0:T(128)} %bitcast.refs_0_, bf16[6,1280,512]{2,1,0:T(8,128)(2,1)} %shard_map.37.refs_1_.refs_2_.refs_3_, bf16[6,1280,512]{2,1,0:T(8,128)(2,1)} %shard_map.37.refs_1_.refs_2_.refs_3_, bf16[6,1280,512]{2,1,0:T(8,128)(2,1)} %shard_map.37.refs_1_.refs_2_.refs_3_, bf16[960,1024]{1,0:T(8,128)(2,1)} %bitcast.4, ...), custom_call_target="tpu_custom_call" | custom-call | tf_op jit(solution)/shard_map/pallas_call | solution.py:257

commit v3 on v2

v3 whole, which is shorter than its diff:
```python
import math

import jax
import jax.numpy as jnp
from jax import lax
from jax.experimental import pallas as pl
from jax.experimental.pallas import tpu as pltpu
from jax.sharding import PartitionSpec as P

D = 1024
HEADS = 16
TH = 40
TW = 24
HALO = 2
HD = 64
OWN = TH * TW
CORNER = 16
SIDE = TH * HALO
CAP = HALO * TW
RIM = 2 * SIDE + 2 * CAP + 4 * CORNER
KEYS = OWN + RIM
CHUNK = 1024
CHUNKS = 3 * D // CHUNK
QS = D // CHUNK
PAD = 1024
FIRST = 896
BLOCKS = ((0, 512), (512, FIRST))
COLS = 256
STEP = 4
PAIRS = HEADS // 2
SCALE = HD ** (-0.5) * math.log2(math.e)
SMALL = 2.0 ** -60
LARGE = 2.0 ** 100
MESH = pl.DeviceIdType.MESH
F32 = jnp.float32
BF16 = jnp.bfloat16

LEFT, RIGHT, TOP, BOTTOM = 0, SIDE, 2 * SIDE, 2 * SIDE + CAP
CORNERS = 2 * SIDE + 2 * CAP


def picked_rows():
    i = lax.broadcasted_iota(jnp.int32, (2 * SIDE + 4 * CORNER, OWN), 0)
    side = jnp.where(i >= SIDE, i - SIDE, i)
    side_row = (side // 2) * TW + side % 2 + jnp.where(i >= SIDE, TW - HALO, 0)
    j = i - 2 * SIDE
    which = j // CORNER
    c = j % 4
    corner_row = (
        (c // 2) * TW + c % 2 + (which % 2) * (TW - HALO) + (which // 2) * (OWN - CAP)
    )
    return jnp.where(i < 2 * SIDE, side_row, corner_row)


def rim_mask(lat, lats, first, shape, dim=0):
    i = lax.broadcasted_iota(jnp.int32, shape, dim) + (first - OWN)
    corner = (i - CORNERS) // CORNER
    in_corner = i >= CORNERS
    upper = ((i >= TOP) & (i < BOTTOM)) | (in_corner & (corner < 2))
    lower = ((i >= BOTTOM) & (i < CORNERS)) | (in_corner & (corner >= 2))
    bad = in_corner & ((i - CORNERS) % CORNER >= 4)
    bad = bad | (upper & (lat == 0)) | (lower & (lat == lats - 1))
    return jnp.where(bad, 0.0, 1.0).astype(F32)


def project_kernel(lats, lons, tok_hbm, w_hbm, qs, ks, vs,
                   tok, normed, w, edge, tok_sem, w_sem, send_sem, recv_sem):
    lat, lon = lax.axis_index("lat"), lax.axis_index("lon")
    up, down = lax.rem(lat + lats - 1, lats), lax.rem(lat + 1, lats)
    west, east = lax.rem(lon + lons - 1, lons), lax.rem(lon + 1, lons)
    barrier = pltpu.get_barrier_semaphore()
    around = [(lat, west), (lat, east), (up, lon), (down, lon),
              (up, west), (up, east), (down, west), (down, east)]
    for device in around:
        pl.semaphore_signal(barrier, inc=1, device_id=device, device_id_type=MESH)

    rows = 320

    def tok_copy(i):
        part = pl.ds(pl.multiple_of(i * rows, rows), rows)
        return pltpu.make_async_copy(tok_hbm.at[part], tok.at[part], tok_sem.at[i])

    for i in range(OWN // rows):
        tok_copy(i).start()

    def w_copy(c):
        at = pl.ds(pl.multiple_of(c * CHUNK, CHUNK), CHUNK)
        return pltpu.make_async_copy(w_hbm.at[:, at], w.at[c], w_sem.at[c])

    for c in range(CHUNKS):
        w_copy(c).start()

    def norm(i, carry):
        tok_copy(i).wait()
        part = pl.ds(pl.multiple_of(i * rows, rows), rows)
        x = tok[part, :].astype(F32)
        centered = x - jnp.mean(x, axis=-1, keepdims=True)
        var = jnp.mean(centered * centered, axis=-1, keepdims=True)
        normed[part, :] = (centered * lax.rsqrt(var + 1e-05)).astype(BF16)
        return carry

    lax.fori_loop(0, OWN // rows, norm, 0)

    take = (picked_rows() == lax.broadcasted_iota(jnp.int32, (2 * SIDE + 4 * CORNER, OWN), 1))
    take = jnp.where(take, 1.0, 0.0).astype(BF16)
    for c in range(2):
        cols = slice(c * 512, c * 512 + 512)
        edge[:, cols] = jnp.dot(take, normed[0:OWN, cols], preferred_element_type=F32).astype(BF16)

    pl.semaphore_wait(barrier, 8)
    e0 = 2 * SIDE
    plan = [
        (edge.at[pl.ds(0, SIDE)], RIGHT, SIDE),
        (edge.at[pl.ds(SIDE, SIDE)], LEFT, SIDE),
        (normed.at[pl.ds(0, CAP)], BOTTOM, CAP),
        (normed.at[pl.ds(OWN - CAP, CAP)], TOP, CAP),
        (edge.at[pl.ds(e0, CORNER)], CORNERS + 3 * CORNER, CORNER),
        (edge.at[pl.ds(e0 + CORNER, CORNER)], CORNERS + 2 * CORNER, CORNER),
        (edge.at[pl.ds(e0 + 2 * CORNER, CORNER)], CORNERS + CORNER, CORNER),
        (edge.at[pl.ds(e0 + 3 * CORNER, CORNER)], CORNERS, CORNER),
    ]
    sends = []
    for n, ((src, at, size), device) in enumerate(zip(plan, around)):
        copy = pltpu.make_async_remote_copy(
            src_ref=src, dst_ref=normed.at[pl.ds(OWN + at, size)],
            send_sem=send_sem.at[n], recv_sem=recv_sem.at[n],
            device_id=device, device_id_type=MESH)
        copy.start()
        sends.append(copy)

    def put_q(y, at):
        t = (y * SCALE).T.astype(BF16)
        for h in range(HEADS):
            low = h % 2 * HD
            qs[h, low:low + HD, at] = t[h * HD:h * HD + HD, :]

    def put_k(y, at):
        y = y.astype(BF16)
        for p in range(PAIRS):
            ks[p, at, :] = y[:, p * 128:p * 128 + 128]

    def put_v(y, at):
        t = y.T.astype(BF16)
        for h in range(HEADS):
            vs[h, 0:HD, at] = t[h * HD:h * HD + HD, :]

    for c, put in ((0, put_q), (1, put_k), (2, put_v)):
        w_copy(c).wait()
        for lo, hi in BLOCKS:
            put(jnp.dot(normed[lo:hi, :], w[c], preferred_element_type=F32), slice(lo, hi))

    unit = rim_mask(lat, lats, 0, (16, KEYS), 1).astype(BF16)
    for h in range(HEADS):
        other = (1 - h % 2) * HD
        qs[h, other:other + HD, :] = jnp.zeros((HD, PAD), BF16)
        vs[h, HD:HD + 16, :] = unit

    for copy in sends:
        copy.wait()

    c0 = CORNERS
    stand = normed[0:CAP, :]
    for lo, hi, at_end in ((TOP, BOTTOM, 0), (c0, c0 + 32, 0),
                           (BOTTOM, c0, lats - 1), (c0 + 32, c0 + 64, lats - 1)):
        at = slice(OWN + lo, OWN + hi)
        normed[at, :] = jnp.where(lat == at_end, stand[0:hi - lo], normed[at, :])
    mask = rim_mask(lat, lats, FIRST, (KEYS - FIRST, 128))
    mask = jnp.concatenate([mask] * (D // 128), axis=1)
    y = jnp.dot(normed[FIRST:KEYS, :], w[1], preferred_element_type=F32)
    put_k(y, slice(FIRST, KEYS))
    y = jnp.dot(normed[FIRST:KEYS, :], w[2], preferred_element_type=F32)
    put_v(y * mask, slice(FIRST, KEYS))
    y = jnp.dot(normed[FIRST:PAD, :], w[0], preferred_element_type=F32)
    put_q(y, slice(FIRST, PAD))


def attend_kernel(q_ref, k_ref, v_ref, tok_hbm, wp_hbm, out_hbm,
                  ctx, tok, wp, out, tok_sem, wp_sem, out_sem):
    tok_copy = pltpu.make_async_copy(tok_hbm, tok, tok_sem)
    wp_copy = pltpu.make_async_copy(wp_hbm, wp, wp_sem)
    tok_copy.start()
    wp_copy.start()

    def run(g, with_top):
        fine = jnp.ones((1, COLS), F32)
        units = [(c, h) for j in range(STEP) for c in range(0, PAD, COLS)
                 for h in range(2 * j, 2 * j + 2)]
        halves = {}

        def scores(c, h):
            return jnp.dot(k_ref[g * STEP + h // 2], q_ref[g * 2 * STEP + h, :, c:c + COLS],
                           preferred_element_type=F32)

        def weights(s):
            if with_top:
                s = s - jnp.max(s, axis=0, keepdims=True)
            return jnp.exp2(s).astype(BF16)

        def finish(c, h, p, fine):
            o = jnp.dot(v_ref[g * 2 * STEP + h], p, preferred_element_type=F32)
            total = o[HD:HD + 1, :]
            fine = jnp.where((total >= SMALL) & (total <= LARGE), fine, 0.0)
            halves[h] = o[0:HD, :] * (1.0 / total)
            if h % 2 == 1:
                pair = jnp.concatenate([halves[h - 1], halves[h]], axis=0)
                ctx[g * STEP + h // 2, c:c + COLS, :] = pair.T.astype(BF16)
            return fine

        s = scores(*units[0])
        held = None
        for n, unit in enumerate(units):
            later = scores(*units[n + 1]) if n + 1 < len(units) else None
            p = weights(s)
            if held is not None:
                fine = finish(*units[n - 1], held, fine)
            held, s = p, later
        return finish(*units[-1], held, fine)

    fine = lax.fori_loop(
        0, PAIRS // STEP, lambda g, fine: fine * run(g, False), jnp.ones((1, COLS), F32))

    @pl.when(jnp.logical_not(jnp.min(fine) > 0.5))
    def _():
        def again(g, carry):
            run(g, True)
            return carry

        lax.fori_loop(0, PAIRS // STEP, again, 0)

    tok_copy.wait()
    wp_copy.wait()
    rows = 240
    copies = []
    for n, r in enumerate(range(0, OWN, rows)):
        context = jnp.concatenate([ctx[p, r:r + rows, :] for p in range(PAIRS)], axis=1)
        y = jnp.dot(context, wp[...], preferred_element_type=F32)
        y = y + tok[r:r + rows, :].astype(F32)
        out[r:r + rows, :] = y.astype(BF16)
        part = pl.ds(r, rows)
        copy = pltpu.make_async_copy(out.at[part], out_hbm.at[part], out_sem.at[n])
        copy.start()
        copies.append(copy)
    for copy in copies:
        copy.wait()


def local(lats, lons, tokens, qkv_weight, proj_weight):
    flat = pltpu.with_memory_space_constraint(tokens.reshape(OWN, D), pltpu.HBM)
    any_spec = pl.BlockSpec(memory_space=pl.ANY)
    vm = pltpu.VMEM
    dma = pltpu.SemaphoreType.DMA
    in_vmem = pl.BlockSpec(memory_space=vm)
    q, k, v = pl.pallas_call(
        lambda *refs: project_kernel(lats, lons, *refs),
        out_shape=[
            vm((HEADS, 2 * HD, PAD), BF16), vm((PAIRS, KEYS, 128), BF16),
            vm((HEADS, HD + 16, KEYS), BF16),
        ],
        in_specs=[any_spec, any_spec],
        out_specs=[in_vmem] * 3,
        scratch_shapes=[
            vm((OWN, D), BF16), vm((KEYS, D), BF16), vm((CHUNKS, D, CHUNK), BF16),
            vm((2 * SIDE + 4 * CORNER, D), BF16),
            dma((OWN // 320,)), dma((CHUNKS,)), dma((8,)), dma((8,)),
        ],
        compiler_params=pltpu.CompilerParams(
            collective_id=0, has_side_effects=True, vmem_limit_bytes=40 * 2 ** 20),
    )(flat, qkv_weight)
    q, k, v = (pltpu.with_memory_space_constraint(x, vm) for x in (q, k, v))
    mixed = pl.pallas_call(
        attend_kernel,
        out_shape=jax.ShapeDtypeStruct((OWN, D), BF16),
        in_specs=[in_vmem] * 3 + [any_spec] * 2,
        out_specs=any_spec,
        scratch_shapes=[
            vm((PAIRS, PAD, 128), BF16), vm((OWN, D), BF16), vm((D, D), BF16),
            vm((OWN, D), BF16), dma(()), dma(()), dma((4,)),
        ],
        compiler_params=pltpu.CompilerParams(vmem_limit_bytes=40 * 2 ** 20),
    )(q, k, v, flat, proj_weight)
    return mixed.reshape(TH, TW, D)


def solution(mesh):
    lats, lons = mesh.shape["lat"], mesh.shape["lon"]
    return jax.shard_map(
        lambda *args: local(lats, lons, *args), mesh=mesh,
        in_specs=(P("lat", "lon", None), P(), P()), out_specs=P("lat", "lon", None),
        check_vma=False)
```

time: 82.2 us -> 62.9 us (0.77)
  Pallas kernels: 81.7 us -> 62.3 us
    pallas_call x1, Pallas kernels: 62.3 us -> 43.8 us  [local(): pl.pallas_call(attend_kernel, out_shape=jax.ShapeDtypeStruct((OWN, D), BF...]
    pallas_call x1, Pallas kernels: 19.4 us -> 18.5 us  [local(): pl.pallas_call(lambda *refs: project_kernel(lats, lons, *refs), out_shape...]
where the time goes in v3:
time: 62.9 us; the launch traced here: 62.4 us
  Pallas kernels  62.3 us (99%)
    pallas_call x1, Pallas kernels, local(): pl.pallas_call(attend_kernel, out_shape=jax.ShapeDtypeStruct((OWN, D), BF...  43.8 us
    pallas_call x1, Pallas kernels, local(): pl.pallas_call(lambda *refs: project_kernel(lats, lons, *refs), out_shape...  18.5 us

profile of v3, /device:TPU:2, one launch (start us, length us, event | category | flops | bytes accessed | tf_op | source)
XLA Modules:
  0.0 62.4 jit_solution(9904913714852489352)
XLA Ops:
  0.0 0.0 copy-start
  0.0 18.5 %shard_map.37 = (bf16[16,128,1024]{2,1,0:T(8,128)(2,1)S(1)}, bf16[8,1280,128]{2,1,0:T(8,128)(2,1)S(1)}, bf16[16,80,1280]{2,1,0:T(8,128)(2,1)S(1)}) custom-call(bf16[960,1024]{1,0:T(8,128)(2,1)} %bitcast.2, bf16[1024,3072]{1,0:T(8,128)(2,1)} %refs_1_.1), custom_call_target="tpu_custom_call" | custom-call | tf_op jit(solution)/shard_map/pallas_call | solution.py:253
  18.5 0.0 copy-done
  18.5 43.8 %shard_map.38 = bf16[960,1024]{1,0:T(8,128)(2,1)} custom-call(bf16[16,128,1024]{2,1,0:T(8,128)(2,1)S(1)} %get-tuple-element.8.q_ref, bf16[8,1280,128]{2,1,0:T(8,128)(2,1)S(1)} %get-tuple-element.9.k_ref, bf16[16,80,1280]{2,1,0:T(8,128)(2,1)S(1)} %get-tuple-element.10.v_ref, bf16[960,1024]{1,0:T(8,128)(2,1)} %bitcast.3, bf16[1024,1024]{1,0:T(8,128)(2,1)S(1)} %copy-done), custom_call_target="tpu_custom_call" | custom-call | tf_op jit(solution)/shard_map/pallas_call | solution.py:270
Async XLA Ops:
  0.0 18.5 %copy-start = (bf16[1024,1024]{1,0:T(8,128)(2,1)S(1)}, bf16[1024,1024]{1,0:T(8,128)(2,1)}, u32[]{:S(2)}) copy-start(bf16[1024,1024]{1,0:T(8,128)(2,1)} %wp_hbm.1) | copy-start | bytes 6291460

commit v4 on v3

--- a/solution.py
+++ b/solution.py
@@ -1,3 +1,4 @@
+import functools
 import math
 
 import jax
@@ -25,6 +26,8 @@
 PAD = 1024
 FIRST = 896
 BLOCKS = ((0, 512), (512, FIRST))
+Q_BLOCKS = ((0, 512), (512, OWN))
+EARLY = 768
 COLS = 256
 STEP = 4
 PAIRS = HEADS // 2
@@ -63,7 +66,36 @@
     return jnp.where(bad, 0.0, 1.0).astype(F32)
 
 
-def project_kernel(lats, lons, tok_hbm, w_hbm, qs, ks, vs,
+def attend(q_ref, k_ref, v_ref, g, step, keys, with_top, finish):
+    units = [(c, h) for j in range(step) for c in range(0, PAD, COLS)
+             for h in range(2 * j, 2 * j + 2)]
+
+    def scores(c, h):
+        return jnp.dot(k_ref[g * step + h // 2, keys, :], q_ref[g * 2 * step + h, :, c:c + COLS],
+                       preferred_element_type=F32)
+
+    def weights(s):
+        if with_top:
+            s = s - jnp.max(s, axis=0, keepdims=True)
+        return jnp.exp2(s).astype(BF16)
+
+    def context(unit, p):
+        c, h = unit
+        o = jnp.dot(v_ref[g * 2 * step + h, :, keys], p, preferred_element_type=F32)
+        finish(g * 2 * step + h, g * step + h // 2, h % 2, slice(c, c + COLS), o)
+
+    s = scores(*units[0])
+    held = None
+    for n, unit in enumerate(units):
+        later = scores(*units[n + 1]) if n + 1 < len(units) else None
+        p = weights(s)
+        if held is not None:
+            context(units[n - 1], held)
+        held, s = p, later
+    context(units[-1], held)
+
+
+def project_kernel(lats, lons, tok_hbm, w_hbm, qs, ks, vs, early,
                    tok, normed, w, edge, tok_sem, w_sem, send_sem, recv_sem):
     lat, lon = lax.axis_index("lat"), lax.axis_index("lon")
     up, down = lax.rem(lat + lats - 1, lats), lax.rem(lat + 1, lats)
@@ -71,8 +103,19 @@
     barrier = pltpu.get_barrier_semaphore()
     around = [(lat, west), (lat, east), (up, lon), (down, lon),
               (up, west), (up, east), (down, west), (down, east)]
-    for device in around:
-        pl.semaphore_signal(barrier, inc=1, device_id=device, device_id_type=MESH)
+    above, below = lat > 0, lat < lats - 1
+    there = [None, None, above, below, above, above, below, below]
+    behind = [None, None, below, above, below, below, above, above]
+
+    def where_there(condition, action):
+        if condition is None:
+            action()
+        else:
+            pl.when(condition)(action)
+
+    for device, condition in zip(around, there):
+        where_there(condition, functools.partial(
+            pl.semaphore_signal, barrier, inc=1, device_id=device, device_id_type=MESH))
 
     rows = 320
 
@@ -107,7 +150,7 @@
         cols = slice(c * 512, c * 512 + 512)
         edge[:, cols] = jnp.dot(take, normed[0:OWN, cols], preferred_element_type=F32).astype(BF16)
 
-    pl.semaphore_wait(barrier, 8)
+    pl.semaphore_wait(barrier, 2 + 3 * above.astype(jnp.int32) + 3 * below.astype(jnp.int32))
     e0 = 2 * SIDE
     plan = [
         (edge.at[pl.ds(0, SIDE)], RIGHT, SIDE),
@@ -125,7 +168,7 @@
             src_ref=src, dst_ref=normed.at[pl.ds(OWN + at, size)],
             send_sem=send_sem.at[n], recv_sem=recv_sem.at[n],
             device_id=device, device_id_type=MESH)
-        copy.start()
+        where_there(there[n], copy.start)
         sends.append(copy)
 
     def put_q(y, at):
@@ -144,88 +187,81 @@
         for h in range(HEADS):
             vs[h, 0:HD, at] = t[h * HD:h * HD + HD, :]
 
-    for c, put in ((0, put_q), (1, put_k), (2, put_v)):
+    for c, put, blocks in ((0, put_q, Q_BLOCKS), (1, put_k, BLOCKS), (2, put_v, BLOCKS)):
         w_copy(c).wait()
-        for lo, hi in BLOCKS:
+        for lo, hi in blocks:
             put(jnp.dot(normed[lo:hi, :], w[c], preferred_element_type=F32), slice(lo, hi))
 
     unit = rim_mask(lat, lats, 0, (16, KEYS), 1).astype(BF16)
     for h in range(HEADS):
         other = (1 - h % 2) * HD
         qs[h, other:other + HD, :] = jnp.zeros((HD, PAD), BF16)
+        qs[h, h % 2 * HD:h % 2 * HD + HD, OWN:PAD] = jnp.zeros((HD, PAD - OWN), BF16)
         vs[h, HD:HD + 16, :] = unit
 
-    for copy in sends:
-        copy.wait()
+    def first_keys(g, carry):
+        def finish(head, pair, odd, cols, o):
+            early[head, :, cols] = o
+
+        attend(qs, ks, vs, g, STEP, slice(0, EARLY), False, finish)
+        return carry
+
+    lax.fori_loop(0, PAIRS // STEP, first_keys, 0)
+
+    for n, copy in enumerate(sends):
+        where_there(there[n], copy.wait_send)
+        where_there(behind[n], copy.wait_recv)
 
     c0 = CORNERS
     stand = normed[0:CAP, :]
     for lo, hi, at_end in ((TOP, BOTTOM, 0), (c0, c0 + 32, 0),
                            (BOTTOM, c0, lats - 1), (c0 + 32, c0 + 64, lats - 1)):
-        at = slice(OWN + lo, OWN + hi)
-        normed[at, :] = jnp.where(lat == at_end, stand[0:hi - lo], normed[at, :])
+        def fill(lo=lo, hi=hi):
+            normed[OWN + lo:OWN + hi, :] = stand[0:hi - lo]
+
+        pl.when(lat == at_end)(fill)
     mask = rim_mask(lat, lats, FIRST, (KEYS - FIRST, 128))
     mask = jnp.concatenate([mask] * (D // 128), axis=1)
     y = jnp.dot(normed[FIRST:KEYS, :], w[1], preferred_element_type=F32)
     put_k(y, slice(FIRST, KEYS))
     y = jnp.dot(normed[FIRST:KEYS, :], w[2], preferred_element_type=F32)
     put_v(y * mask, slice(FIRST, KEYS))
-    y = jnp.dot(normed[FIRST:PAD, :], w[0], preferred_element_type=F32)
-    put_q(y, slice(FIRST, PAD))
-
-
-def attend_kernel(q_ref, k_ref, v_ref, tok_hbm, wp_hbm, out_hbm,
+
+
+def attend_kernel(q_ref, k_ref, v_ref, early, tok_hbm, wp_hbm, out_hbm,
                   ctx, tok, wp, out, tok_sem, wp_sem, out_sem):
     tok_copy = pltpu.make_async_copy(tok_hbm, tok, tok_sem)
     wp_copy = pltpu.make_async_copy(wp_hbm, wp, wp_sem)
     tok_copy.start()
     wp_copy.start()
 
-    def run(g, with_top):
-        fine = jnp.ones((1, COLS), F32)
-        units = [(c, h) for j in range(STEP) for c in range(0, PAD, COLS)
-                 for h in range(2 * j, 2 * j + 2)]
-        halves = {}
-
-        def scores(c, h):
-            return jnp.dot(k_ref[g * STEP + h // 2], q_ref[g * 2 * STEP + h, :, c:c + COLS],
-                           preferred_element_type=F32)
-
-        def weights(s):
-            if with_top:
-                s = s - jnp.max(s, axis=0, keepdims=True)
-            return jnp.exp2(s).astype(BF16)
-
-        def finish(c, h, p, fine):
-            o = jnp.dot(v_ref[g * 2 * STEP + h], p, preferred_element_type=F32)
+    def run(g, step, with_top):
+        state = [jnp.ones((1, COLS), F32), None]
+
+        def finish(head, pair, odd, cols, o):
+            if not with_top:
+                o = o + early[head, :, cols]
             total = o[HD:HD + 1, :]
-            fine = jnp.where((total >= SMALL) & (total <= LARGE), fine, 0.0)
-            halves[h] = o[0:HD, :] * (1.0 / total)
-            if h % 2 == 1:
-                pair = jnp.concatenate([halves[h - 1], halves[h]], axis=0)
-                ctx[g * STEP + h // 2, c:c + COLS, :] = pair.T.astype(BF16)
-            return fine
-
-        s = scores(*units[0])
-        held = None
-        for n, unit in enumerate(units):
-            later = scores(*units[n + 1]) if n + 1 < len(units) else None
-            p = weights(s)
-            if held is not None:
-                fine = finish(*units[n - 1], held, fine)
-            held, s = p, later
-        return finish(*units[-1], held, fine)
+            state[0] = jnp.where((total >= SMALL) & (total <= LARGE), state[0], 0.0)
+            half = o[0:HD, :] * (1.0 / total)
+            if odd:
+                ctx[pair, cols, :] = jnp.concatenate([state[1], half], axis=0).T.astype(BF16)
+            state[1] = half
+
+        keys = slice(0 if with_top else EARLY, KEYS)
+        attend(q_ref, k_ref, v_ref, g, step, keys, with_top, finish)
+        return state[0]
 
     fine = lax.fori_loop(
-        0, PAIRS // STEP, lambda g, fine: fine * run(g, False), jnp.ones((1, COLS), F32))
+        0, PAIRS // STEP, lambda g, fine: fine * run(g, STEP, False), jnp.ones((1, COLS), F32))
 
     @pl.when(jnp.logical_not(jnp.min(fine) > 0.5))
     def _():
         def again(g, carry):
-            run(g, True)
+            run(g, 1, True)
             return carry
 
-        lax.fori_loop(0, PAIRS // STEP, again, 0)
+        lax.fori_loop(0, PAIRS, again, 0)
 
     tok_copy.wait()
     wp_copy.wait()
@@ -250,14 +286,14 @@
     vm = pltpu.VMEM
     dma = pltpu.SemaphoreType.DMA
     in_vmem = pl.BlockSpec(memory_space=vm)
-    q, k, v = pl.pallas_call(
+    results = pl.pallas_call(
         lambda *refs: project_kernel(lats, lons, *refs),
         out_shape=[
             vm((HEADS, 2 * HD, PAD), BF16), vm((PAIRS, KEYS, 128), BF16),
-            vm((HEADS, HD + 16, KEYS), BF16),
+            vm((HEADS, HD + 16, KEYS), BF16), vm((HEADS, HD + 16, PAD), F32),
         ],
         in_specs=[any_spec, any_spec],
-        out_specs=[in_vmem] * 3,
+        out_specs=[in_vmem] * 4,
         scratch_shapes=[
             vm((OWN, D), BF16), vm((KEYS, D), BF16), vm((CHUNKS, D, CHUNK), BF16),
             vm((2 * SIDE + 4 * CORNER, D), BF16),
@@ -266,18 +302,18 @@
         compiler_params=pltpu.CompilerParams(
             collective_id=0, has_side_effects=True, vmem_limit_bytes=40 * 2 ** 20),
     )(flat, qkv_weight)
-    q, k, v = (pltpu.with_memory_space_constraint(x, vm) for x in (q, k, v))
+    results = [pltpu.with_memory_space_constraint(x, vm) for x in results]
     mixed = pl.pallas_call(
         attend_kernel,
         out_shape=jax.ShapeDtypeStruct((OWN, D), BF16),
-        in_specs=[in_vmem] * 3 + [any_spec] * 2,
+        in_specs=[in_vmem] * 4 + [any_spec] * 2,
         out_specs=any_spec,
         scratch_shapes=[
             vm((PAIRS, PAD, 128), BF16), vm((OWN, D), BF16), vm((D, D), BF16),
             vm((OWN, D), BF16), dma(()), dma(()), dma((4,)),
         ],
         compiler_params=pltpu.CompilerParams(vmem_limit_bytes=40 * 2 ** 20),
-    )(q, k, v, flat, proj_weight)
+    )(*results, flat, proj_weight)
     return mixed.reshape(TH, TW, D)
 
 

time: 62.9 us -> 65.7 us (1.045)
  Pallas kernels: 62.3 us -> 65.5 us
    pallas_call x1, Pallas kernels: 18.5 us -> 28 us  [local(): pl.pallas_call(lambda *refs: project_kernel(lats, lons, *refs), out_shape...]
    pallas_call x1, Pallas kernels: 43.8 us -> 37.5 us  [local(): pl.pallas_call(attend_kernel, out_shape=jax.ShapeDtypeStruct((OWN, D), BF...]
where the time goes in v4:
time: 65.7 us; the launch traced here: 65.6 us
  Pallas kernels  65.5 us (100%)
    pallas_call x1, Pallas kernels, local(): pl.pallas_call(attend_kernel, out_shape=jax.ShapeDtypeStruct((OWN, D), BF...  37.5 us
    pallas_call x1, Pallas kernels, local(): pl.pallas_call(lambda *refs: project_kernel(lats, lons, *refs), out_shape...  28 us

profile of v4, /device:TPU:2, one launch (start us, length us, event | category | flops | bytes accessed | tf_op | source)
XLA Modules:
  0.0 65.6 jit_solution(7931827772664355880)
XLA Ops:
  0.0 28.0 %shard_map.37 = (bf16[16,128,1024]{2,1,0:T(8,128)(2,1)S(1)}, bf16[8,1280,128]{2,1,0:T(8,128)(2,1)S(1)}, bf16[16,80,1280]{2,1,0:T(8,128)(2,1)S(1)}, f32[16,80,1024]{2,1,0:T(8,128)S(1)}) custom-call(bf16[960,1024]{1,0:T(8,128)(2,1)} %bitcast.2, bf16[1024,3072]{1,0:T(8,128)(2,1)} %refs_1_.1), custom_call_target="tpu_custom_call" | custom-call | tf_op jit(solution)/shard_map/pallas_call | solution.py:289
  28.0 37.5 %shard_map.38 = bf16[960,1024]{1,0:T(8,128)(2,1)} custom-call(bf16[16,128,1024]{2,1,0:T(8,128)(2,1)S(1)} %get-tuple-element.9.q_ref, bf16[8,1280,128]{2,1,0:T(8,128)(2,1)S(1)} %get-tuple-element.10.k_ref, bf16[16,80,1280]{2,1,0:T(8,128)(2,1)S(1)} %get-tuple-element.11.v_ref, f32[16,80,1024]{2,1,0:T(8,128)S(1)} %get-tuple-element.12.early, ...), custom_call_target="tpu_custom_call" | custom-call | tf_op jit(solution)/shard_map/pallas_call | solution.py:306

commit v5 on v4

--- a/solution.py
+++ b/solution.py
@@ -150,27 +150,6 @@
         cols = slice(c * 512, c * 512 + 512)
         edge[:, cols] = jnp.dot(take, normed[0:OWN, cols], preferred_element_type=F32).astype(BF16)
 
-    pl.semaphore_wait(barrier, 2 + 3 * above.astype(jnp.int32) + 3 * below.astype(jnp.int32))
-    e0 = 2 * SIDE
-    plan = [
-        (edge.at[pl.ds(0, SIDE)], RIGHT, SIDE),
-        (edge.at[pl.ds(SIDE, SIDE)], LEFT, SIDE),
-        (normed.at[pl.ds(0, CAP)], BOTTOM, CAP),
-        (normed.at[pl.ds(OWN - CAP, CAP)], TOP, CAP),
-        (edge.at[pl.ds(e0, CORNER)], CORNERS + 3 * CORNER, CORNER),
-        (edge.at[pl.ds(e0 + CORNER, CORNER)], CORNERS + 2 * CORNER, CORNER),
-        (edge.at[pl.ds(e0 + 2 * CORNER, CORNER)], CORNERS + CORNER, CORNER),
-        (edge.at[pl.ds(e0 + 3 * CORNER, CORNER)], CORNERS, CORNER),
-    ]
-    sends = []
-    for n, ((src, at, size), device) in enumerate(zip(plan, around)):
-        copy = pltpu.make_async_remote_copy(
-            src_ref=src, dst_ref=normed.at[pl.ds(OWN + at, size)],
-            send_sem=send_sem.at[n], recv_sem=recv_sem.at[n],
-            device_id=device, device_id_type=MESH)
-        where_there(there[n], copy.start)
-        sends.append(copy)
-
     def put_q(y, at):
         t = (y * SCALE).T.astype(BF16)
         for h in range(HEADS):
@@ -187,7 +166,32 @@
         for h in range(HEADS):
             vs[h, 0:HD, at] = t[h * HD:h * HD + HD, :]
 
+    sends = []
+
+    def send():
+        pl.semaphore_wait(barrier, 2 + 3 * above.astype(jnp.int32) + 3 * below.astype(jnp.int32))
+        e0 = 2 * SIDE
+        plan = [
+            (edge.at[pl.ds(0, SIDE)], RIGHT, SIDE),
+            (edge.at[pl.ds(SIDE, SIDE)], LEFT, SIDE),
+            (normed.at[pl.ds(0, CAP)], BOTTOM, CAP),
+            (normed.at[pl.ds(OWN - CAP, CAP)], TOP, CAP),
+            (edge.at[pl.ds(e0, CORNER)], CORNERS + 3 * CORNER, CORNER),
+            (edge.at[pl.ds(e0 + CORNER, CORNER)], CORNERS + 2 * CORNER, CORNER),
+            (edge.at[pl.ds(e0 + 2 * CORNER, CORNER)], CORNERS + CORNER, CORNER),
+            (edge.at[pl.ds(e0 + 3 * CORNER, CORNER)], CORNERS, CORNER),
+        ]
+        for n, ((src, at, size), device) in enumerate(zip(plan, around)):
+            copy = pltpu.make_async_remote_copy(
+                src_ref=src, dst_ref=normed.at[pl.ds(OWN + at, size)],
+                send_sem=send_sem.at[n], recv_sem=recv_sem.at[n],
+                device_id=device, device_id_type=MESH)
+            where_there(there[n], copy.start)
+            sends.append(copy)
+
     for c, put, blocks in ((0, put_q, Q_BLOCKS), (1, put_k, BLOCKS), (2, put_v, BLOCKS)):
+        if c == 2:
+            send()
         w_copy(c).wait()
         for lo, hi in blocks:
             put(jnp.dot(normed[lo:hi, :], w[c], preferred_element_type=F32), slice(lo, hi))

time: 65.7 us -> 61.3 us (0.933)
  Pallas kernels: 65.5 us -> 61.1 us
    pallas_call x1, Pallas kernels: 28 us -> 23.6 us  [local(): pl.pallas_call(lambda *refs: project_kernel(lats, lons, *refs), out_shape...]
where the time goes in v5:
time: 61.3 us; the launch traced here: 61.2 us
  Pallas kernels  61.1 us (100%)
    pallas_call x1, Pallas kernels, local(): pl.pallas_call(attend_kernel, out_shape=jax.ShapeDtypeStruct((OWN, D), BF...  37.5 us
    pallas_call x1, Pallas kernels, local(): pl.pallas_call(lambda *refs: project_kernel(lats, lons, *refs), out_shape...  23.6 us

profile of v5, /device:TPU:2, one launch (start us, length us, event | category | flops | bytes accessed | tf_op | source)
XLA Modules:
  0.0 61.2 jit_solution(957813455583031479)
XLA Ops:
  0.0 23.6 %shard_map.37 = (bf16[16,128,1024]{2,1,0:T(8,128)(2,1)S(1)}, bf16[8,1280,128]{2,1,0:T(8,128)(2,1)S(1)}, bf16[16,80,1280]{2,1,0:T(8,128)(2,1)S(1)}, f32[16,80,1024]{2,1,0:T(8,128)S(1)}) custom-call(bf16[960,1024]{1,0:T(8,128)(2,1)} %bitcast.2, bf16[1024,3072]{1,0:T(8,128)(2,1)} %refs_1_.1), custom_call_target="tpu_custom_call" | custom-call | tf_op jit(solution)/shard_map/pallas_call | solution.py:293
  23.6 37.5 %shard_map.38 = bf16[960,1024]{1,0:T(8,128)(2,1)} custom-call(bf16[16,128,1024]{2,1,0:T(8,128)(2,1)S(1)} %get-tuple-element.9.q_ref, bf16[8,1280,128]{2,1,0:T(8,128)(2,1)S(1)} %get-tuple-element.10.k_ref, bf16[16,80,1280]{2,1,0:T(8,128)(2,1)S(1)} %get-tuple-element.11.v_ref, f32[16,80,1024]{2,1,0:T(8,128)S(1)} %get-tuple-element.12.early, ...), custom_call_target="tpu_custom_call" | custom-call | tf_op jit(solution)/shard_map/pallas_call | solution.py:310

commit v6 on v5

--- a/solution.py
+++ b/solution.py
@@ -43,7 +43,7 @@
 
 
 def picked_rows():
-    i = lax.broadcasted_iota(jnp.int32, (2 * SIDE + 4 * CORNER, OWN), 0)
+    i = lax.broadcasted_iota(jnp.int32, (2 * SIDE + 4 * CORNER, 1), 0)
     side = jnp.where(i >= SIDE, i - SIDE, i)
     side_row = (side // 2) * TW + side % 2 + jnp.where(i >= SIDE, TW - HALO, 0)
     j = i - 2 * SIDE
@@ -132,6 +132,13 @@
 
     for c in range(CHUNKS):
         w_copy(c).start()
+
+    unit = rim_mask(lat, lats, 0, (16, KEYS), 1).astype(BF16)
+    for h in range(HEADS):
+        other = (1 - h % 2) * HD
+        qs[h, other:other + HD, :] = jnp.zeros((HD, PAD), BF16)
+        qs[h, h % 2 * HD:h % 2 * HD + HD, OWN:PAD] = jnp.zeros((HD, PAD - OWN), BF16)
+        vs[h, HD:HD + 16, :] = unit
 
     def norm(i, carry):
         tok_copy(i).wait()
@@ -195,13 +202,6 @@
         w_copy(c).wait()
         for lo, hi in blocks:
             put(jnp.dot(normed[lo:hi, :], w[c], preferred_element_type=F32), slice(lo, hi))
-
-    unit = rim_mask(lat, lats, 0, (16, KEYS), 1).astype(BF16)
-    for h in range(HEADS):
-        other = (1 - h % 2) * HD
-        qs[h, other:other + HD, :] = jnp.zeros((HD, PAD), BF16)
-        qs[h, h % 2 * HD:h % 2 * HD + HD, OWN:PAD] = jnp.zeros((HD, PAD - OWN), BF16)
-        vs[h, HD:HD + 16, :] = unit
 
     def first_keys(g, carry):
         def finish(head, pair, odd, cols, o):

time: 61.3 us -> 61.1 us (level)
  no operation moved by 1% of the time
where the time goes in v6:
time: 61.1 us; the launch traced here: 61 us
  Pallas kernels  60.8 us (100%)
    pallas_call x1, Pallas kernels, local(): pl.pallas_call(attend_kernel, out_shape=jax.ShapeDtypeStruct((OWN, D), BF...  37.5 us
    pallas_call x1, Pallas kernels, local(): pl.pallas_call(lambda *refs: project_kernel(lats, lons, *refs), out_shape...  23.3 us

profile of v6, /device:TPU:2, one launch (start us, length us, event | category | flops | bytes accessed | tf_op | source)
XLA Modules:
  0.0 61.0 jit_solution(12543945933854342534)
XLA Ops:
  0.0 23.3 %shard_map.37 = (bf16[16,128,1024]{2,1,0:T(8,128)(2,1)S(1)}, bf16[8,1280,128]{2,1,0:T(8,128)(2,1)S(1)}, bf16[16,80,1280]{2,1,0:T(8,128)(2,1)S(1)}, f32[16,80,1024]{2,1,0:T(8,128)S(1)}) custom-call(bf16[960,1024]{1,0:T(8,128)(2,1)} %bitcast.2, bf16[1024,3072]{1,0:T(8,128)(2,1)} %refs_1_.1), custom_call_target="tpu_custom_call" | custom-call | tf_op jit(solution)/shard_map/pallas_call | solution.py:293
  23.4 37.5 %shard_map.38 = bf16[960,1024]{1,0:T(8,128)(2,1)} custom-call(bf16[16,128,1024]{2,1,0:T(8,128)(2,1)S(1)} %get-tuple-element.9.q_ref, bf16[8,1280,128]{2,1,0:T(8,128)(2,1)S(1)} %get-tuple-element.10.k_ref, bf16[16,80,1280]{2,1,0:T(8,128)(2,1)S(1)} %get-tuple-element.11.v_ref, f32[16,80,1024]{2,1,0:T(8,128)S(1)} %get-tuple-element.12.early, ...), custom_call_target="tpu_custom_call" | custom-call | tf_op jit(solution)/shard_map/pallas_call | solution.py:310

commit v7 on v6

--- a/solution.py
+++ b/solution.py
@@ -197,11 +197,11 @@
             sends.append(copy)
 
     for c, put, blocks in ((0, put_q, Q_BLOCKS), (1, put_k, BLOCKS), (2, put_v, BLOCKS)):
-        if c == 2:
-            send()
         w_copy(c).wait()
         for lo, hi in blocks:
             put(jnp.dot(normed[lo:hi, :], w[c], preferred_element_type=F32), slice(lo, hi))
+            if c == 2 and lo == 0:
+                send()
 
     def first_keys(g, carry):
         def finish(head, pair, odd, cols, o):

time: 61.1 us -> 61 us (level)
  no operation moved by 1% of the time
where the time goes in v7:
time: 61 us; the launch traced here: 60.5 us
  Pallas kernels  60.3 us (99%)
    pallas_call x1, Pallas kernels, local(): pl.pallas_call(attend_kernel, out_shape=jax.ShapeDtypeStruct((OWN, D), BF...  37.5 us
    pallas_call x1, Pallas kernels, local(): pl.pallas_call(lambda *refs: project_kernel(lats, lons, *refs), out_shape...  22.8 us

profile of v7, /device:TPU:2, one launch (start us, length us, event | category | flops | bytes accessed | tf_op | source)
XLA Modules:
  0.0 60.5 jit_solution(13768345841702419090)
XLA Ops:
  0.0 22.8 %shard_map.37 = (bf16[16,128,1024]{2,1,0:T(8,128)(2,1)S(1)}, bf16[8,1280,128]{2,1,0:T(8,128)(2,1)S(1)}, bf16[16,80,1280]{2,1,0:T(8,128)(2,1)S(1)}, f32[16,80,1024]{2,1,0:T(8,128)S(1)}) custom-call(bf16[960,1024]{1,0:T(8,128)(2,1)} %bitcast.2, bf16[1024,3072]{1,0:T(8,128)(2,1)} %refs_1_.1), custom_call_target="tpu_custom_call" | custom-call | tf_op jit(solution)/shard_map/pallas_call | solution.py:293
  22.8 37.5 %shard_map.38 = bf16[960,1024]{1,0:T(8,128)(2,1)} custom-call(bf16[16,128,1024]{2,1,0:T(8,128)(2,1)S(1)} %get-tuple-element.9.q_ref, bf16[8,1280,128]{2,1,0:T(8,128)(2,1)S(1)} %get-tuple-element.10.k_ref, bf16[16,80,1280]{2,1,0:T(8,128)(2,1)S(1)} %get-tuple-element.11.v_ref, f32[16,80,1024]{2,1,0:T(8,128)S(1)} %get-tuple-element.12.early, ...), custom_call_target="tpu_custom_call" | custom-call | tf_op jit(solution)/shard_map/pallas_call | solution.py:310

commit v8 on v6

--- a/solution.py
+++ b/solution.py
@@ -85,14 +85,15 @@
         finish(g * 2 * step + h, g * step + h // 2, h % 2, slice(c, c + COLS), o)
 
     s = scores(*units[0])
-    held = None
+    held = []
     for n, unit in enumerate(units):
         later = scores(*units[n + 1]) if n + 1 < len(units) else None
-        p = weights(s)
-        if held is not None:
-            context(units[n - 1], held)
-        held, s = p, later
-    context(units[-1], held)
+        held.append(weights(s))
+        if n >= 2:
+            context(units[n - 2], held.pop(0))
+        s = later
+    for unit in units[-2:]:
+        context(unit, held.pop(0))
 
 
 def project_kernel(lats, lons, tok_hbm, w_hbm, qs, ks, vs, early,

time: 61.1 us -> 61.1 us (level)
  no operation moved by 1% of the time
where the time goes in v8:
time: 61.1 us; the launch traced here: 61 us
  Pallas kernels  60.9 us (100%)
    pallas_call x1, Pallas kernels, local(): pl.pallas_call(attend_kernel, out_shape=jax.ShapeDtypeStruct((OWN, D), BF...  37.4 us
    pallas_call x1, Pallas kernels, local(): pl.pallas_call(lambda *refs: project_kernel(lats, lons, *refs), out_shape...  23.4 us

profile of v8, /device:TPU:2, one launch (start us, length us, event | category | flops | bytes accessed | tf_op | source)
XLA Modules:
  0.0 61.0 jit_solution(9006834164301623693)
XLA Ops:
  0.0 23.4 %shard_map.37 = (bf16[16,128,1024]{2,1,0:T(8,128)(2,1)S(1)}, bf16[8,1280,128]{2,1,0:T(8,128)(2,1)S(1)}, bf16[16,80,1280]{2,1,0:T(8,128)(2,1)S(1)}, f32[16,80,1024]{2,1,0:T(8,128)S(1)}) custom-call(bf16[960,1024]{1,0:T(8,128)(2,1)} %bitcast.2, bf16[1024,3072]{1,0:T(8,128)(2,1)} %refs_1_.1), custom_call_target="tpu_custom_call" | custom-call | tf_op jit(solution)/shard_map/pallas_call | solution.py:294
  23.4 37.4 %shard_map.38 = bf16[960,1024]{1,0:T(8,128)(2,1)} custom-call(bf16[16,128,1024]{2,1,0:T(8,128)(2,1)S(1)} %get-tuple-element.9.q_ref, bf16[8,1280,128]{2,1,0:T(8,128)(2,1)S(1)} %get-tuple-element.10.k_ref, bf16[16,80,1280]{2,1,0:T(8,128)(2,1)S(1)} %get-tuple-element.11.v_ref, f32[16,80,1024]{2,1,0:T(8,128)S(1)} %get-tuple-element.12.early, ...), custom_call_target="tpu_custom_call" | custom-call | tf_op jit(solution)/shard_map/pallas_call | solution.py:311
